TPU v7x, 1024 devices: a whole 4x4x32 slice. The times are simulated.
1024 devices in a mesh: dp: 16 (over x, y_lo, core), space: 64 (over y_hi, z).
Axes of the slice: x: 4, y: 4 (y_hi: 2, y_lo: 2; y = y_hi * 2 + y_lo), z: 32, core: 2. Of those that a mesh axis runs over, the one named last changes fastest.
Arguments:
- inputs: bfloat16 [16, 64, 24, 4608], P('dp', 'space'), may hold values from -6 to 6
- cotangent: bfloat16 [16, 64, 24, 4608], P('dp', 'space'), may hold values from -16 to 16
- tile_rows: int32 [64], replicated, may hold values from 4 to 24, as said below
- neighbour_step: int32 [64, 4], replicated, may hold values from -1 to 1
- neighbour_code: int32 [64, 4], replicated, may hold values from 0 to 7
- neighbour_shift: int32 [64, 4], replicated, may hold values from -6 to 6
- conv_kernel: float32 [7, 7, 192], replicated, may hold values from -0.875 to 0.875
- conv_bias: float32 [192], replicated, may hold values from -3 to 3
- norm_gain: float32 [192], replicated, may hold values from 0.5 to 1.5
- norm_bias: float32 [192], replicated, may hold values from -3 to 3
- w_expand: bfloat16 [192, 768], replicated, may hold values from -0.4375 to 0.4375
- b_expand: float32 [768], replicated, may hold values from -3 to 3
- w_project: bfloat16 [768, 192], replicated, may hold values from -0.21875 to 0.21875
- b_project: float32 [192], replicated, may hold values from -3 to 3
- layer_scale: float32 [192], replicated, may hold values from 0.5 to 1.5
Outputs:
- outputs: bfloat16 [16, 64, 24, 4608], P('dp', 'space')
- input_grad: bfloat16 [16, 64, 24, 4608], P('dp', 'space')
- weight_grads: float32 [294912], P(('dp', 'space'))
Inputs may be any that keep to these rules, and one draw needn't show every extreme that they name: `tile_rows`: tile t and tile t + 32 hold 28 rows together; tile 0 holds 24 rows.
All inputs are finite; a program needn't handle non-finite values.
Results may differ from a plain program's by a relative error of at most 0.023.
Values may be sent and summed in bfloat16 or wider, within the bound.
A program may use at most 32 MiB of HBM per device.

v0:
```python
import math

import jax
import jax.numpy as jnp
from jax import lax
from jax.sharding import PartitionSpec as P

REACH = 1


root_half = 0.7071067811865476
inv_root_tau = 0.3989422804014327


def from_behind(array, axis, by):
    length = lax.axis_size(axis)
    return lax.ppermute(array, axis, [(i, (i + by) % length) for i in range(length)])


def gelu_exact(values):
    return 0.5 * values * (1.0 + jax.scipy.special.erf(values * root_half))


def gelu_slope(values):
    return 0.5 * (
        1.0 + jax.scipy.special.erf(values * root_half)
    ) + values * inv_root_tau * jnp.exp(-0.5 * values * values)


def tile_bands(tile_field, tile_len):
    tile_side = tile_field.shape[0]
    upper = tile_field[0:3]
    bottom_rows = tile_len - 1 - jnp.arange(3, dtype=jnp.int32)
    bottom = jnp.take(tile_field, bottom_rows, axis=0)
    leftmost = jnp.transpose(tile_field[:, 0:3], (1, 0, 2))
    rightmost = jnp.transpose(tile_field[:, tile_side - 3 :][:, ::-1], (1, 0, 2))
    return jnp.stack([upper, bottom, leftmost, rightmost])


def orient_band(band_rows, orient_code, edge_shift):
    tile_side = band_rows.shape[1]
    flipped = jnp.where(orient_code % 2 == 1, band_rows[:, ::-1], band_rows)
    padded = jnp.pad(flipped, ((0, 0), (tile_side, tile_side), (0, 0)))
    return lax.dynamic_slice_in_dim(padded, tile_side - edge_shift, tile_side, 1)


def restore_band(band_rows, orient_code, edge_shift):
    tile_side = band_rows.shape[1]
    padded = jnp.pad(band_rows, ((0, 0), (tile_side, tile_side), (0, 0)))
    moved = lax.dynamic_slice_in_dim(padded, tile_side + edge_shift, tile_side, 1)
    return jnp.where(orient_code % 2 == 1, moved[:, ::-1], moved)


def extend_tile(tile_field, tile_len, halos):
    tile_side = tile_field.shape[0]
    channels = tile_field.shape[2]
    extended = jnp.zeros((tile_side + 6, tile_side + 6, channels), tile_field.dtype)
    extended = extended.at[3 : tile_side + 3, 3 : tile_side + 3].set(tile_field)
    extended = extended.at[0:3, 3 : tile_side + 3].set(halos[0][::-1])
    extended = extended.at[3 : tile_side + 3, 0:3].set(jnp.transpose(halos[2], (1, 0, 2))[:, ::-1])
    extended = extended.at[3 : tile_side + 3, tile_side + 3 : tile_side + 6].set(
        jnp.transpose(halos[3], (1, 0, 2))
    )
    zero_index = tile_len * 0
    return lax.dynamic_update_slice(extended, halos[1], (tile_len + 3, zero_index + 3, zero_index))


def halo_grads(grad_ext, tile_len):
    tile_side = grad_ext.shape[0] - 6
    channels = grad_ext.shape[2]
    zero_index = tile_len * 0
    upper = grad_ext[0:3, 3 : tile_side + 3][::-1]
    bottom = lax.dynamic_slice(
        grad_ext, (tile_len + 3, zero_index + 3, zero_index), (3, tile_side, channels)
    )
    leftmost = jnp.transpose(grad_ext[3 : tile_side + 3, 0:3][:, ::-1], (1, 0, 2))
    rightmost = jnp.transpose(grad_ext[3 : tile_side + 3, tile_side + 3 : tile_side + 6], (1, 0, 2))
    return jnp.stack([upper, bottom, leftmost, rightmost])


def band_adjoint(grad_bands, tile_len):
    tile_side = grad_bands.shape[2]
    channels = grad_bands.shape[3]
    result = jnp.zeros((tile_side, tile_side, channels), jnp.float32)
    result = result.at[0:3].add(grad_bands[0])
    bottom_rows = tile_len - 1 - jnp.arange(3, dtype=jnp.int32)
    result = result.at[bottom_rows].add(grad_bands[1])
    result = result.at[:, 0:3].add(jnp.transpose(grad_bands[2], (1, 0, 2)))
    result = result.at[:, tile_side - 3 :].add(jnp.transpose(grad_bands[3], (1, 0, 2))[:, ::-1])
    return result


def depthwise(extended, conv_kernel):
    channels = conv_kernel.shape[-1]
    return lax.conv_general_dilated(
        extended[None],
        conv_kernel[:, :, None, :],
        (1, 1),
        "VALID",
        dimension_numbers=("NHWC", "HWIO", "NHWC"),
        feature_group_count=channels,
        precision=lax.Precision.HIGHEST,
    )[0]


def layer_norm(values, norm_gain, norm_bias):
    centred = values - jnp.mean(values, axis=-1, keepdims=True)
    variance = jnp.mean(centred * centred, axis=-1, keepdims=True)
    return centred * lax.rsqrt(variance + 1e-06) * norm_gain + norm_bias


def pointwise(cells, d_cells, w_expand, b_expand, w_project, b_project):
    pre = jnp.dot(cells, w_expand, preferred_element_type=jnp.float32) + b_expand
    act = gelu_exact(pre).astype(jnp.bfloat16)
    branch = (jnp.dot(act, w_project, preferred_element_type=jnp.float32) + b_project).astype(
        jnp.bfloat16
    )
    d_act = lax.dot_general(
        d_cells, w_project, (((1,), (1,)), ((), ())), preferred_element_type=jnp.float32
    )
    d_pre = (d_act * gelu_slope(pre)).astype(jnp.bfloat16)
    d_normed = lax.dot_general(
        d_pre, w_expand, (((1,), (1,)), ((), ())), preferred_element_type=jnp.float32
    ).astype(jnp.bfloat16)
    grad_in = lax.dot_general(
        cells, d_pre, (((0,), (0,)), ((), ())), preferred_element_type=jnp.float32
    )
    grad_proj = lax.dot_general(
        act, d_cells, (((0,), (0,)), ((), ())), preferred_element_type=jnp.float32
    )
    return (branch, d_normed, grad_in, grad_proj)


def nearby_bands(bands):
    pieces = []
    for offset in range(-REACH, REACH + 1):
        if offset == 0:
            pieces.append(bands)
        else:
            pieces.append(from_behind(bands, "space", -offset))
    return jnp.concatenate(pieces, axis=0)


def nearby_adjoints(bands):
    pieces = []
    for offset in range(-REACH, REACH + 1):
        if offset == 0:
            pieces.append(bands)
        else:
            pieces.append(from_behind(bands, "space", -offset))
    return jnp.concatenate(pieces, axis=0)


def local(
    inputs,
    cotangent,
    tile_rows,
    neighbour_step,
    neighbour_code,
    neighbour_shift,
    conv_kernel,
    conv_bias,
    norm_gain,
    norm_bias,
    w_expand,
    b_expand,
    w_project,
    b_project,
    layer_scale,
):
    channels = conv_kernel.shape[-1]
    tile_side = inputs.shape[2]
    tiles = lax.axis_size("space")
    samples = lax.axis_size("dp")
    own_index = lax.axis_index("space")
    tile_len = tile_rows[own_index]
    inside = (jnp.arange(tile_side, dtype=jnp.int32) < tile_len)[:, None, None]
    tile_field = jnp.where(
        inside, inputs[0, 0].reshape(tile_side, tile_side, channels), jnp.zeros((), jnp.bfloat16)
    )
    bands = tile_bands(tile_field, tile_len)
    nearby = nearby_bands(bands.reshape(1, 4, 3, tile_side * channels))
    nearby = nearby.reshape(2 * REACH + 1, 4, 3, tile_side, channels)
    halo_list = []
    for which_side in range(4):
        source = nearby[
            REACH + neighbour_step[own_index, which_side],
            neighbour_code[own_index, which_side] // 2,
        ]
        halo_list.append(
            orient_band(
                source,
                neighbour_code[own_index, which_side],
                neighbour_shift[own_index, which_side],
            )
        )
    extended = extend_tile(tile_field, tile_len, jnp.stack(halo_list)).astype(jnp.float32)
    mixed = depthwise(extended, conv_kernel) + conv_bias
    normed_f, norm_pull = jax.vjp(lambda values: layer_norm(values, norm_gain, norm_bias), mixed)
    normed = normed_f.astype(jnp.bfloat16)
    grad_out = jnp.where(
        inside, cotangent[0, 0].reshape(tile_side, tile_side, channels).astype(jnp.float32), 0.0
    )
    d_branch = (layer_scale * grad_out).astype(jnp.bfloat16)
    branch, d_normed, grad_in, grad_proj = pointwise(
        normed.reshape(-1, channels),
        d_branch.reshape(-1, channels),
        w_expand,
        b_expand,
        w_project,
        b_project,
    )
    branch = branch.reshape(tile_side, tile_side, channels)
    d_normed = d_normed.reshape(tile_side, tile_side, channels)
    outputs = jnp.where(
        inside, tile_field.astype(jnp.float32) + layer_scale * branch.astype(jnp.float32), 0.0
    )
    d_mixed = norm_pull(d_normed.astype(jnp.float32))[0]
    conv_pull = jax.vjp(lambda values: depthwise(values, conv_kernel), extended)[1]
    grad_ext = conv_pull(d_mixed)[0]
    grad_halos = halo_grads(grad_ext, tile_len)
    returned = jax.vmap(restore_band)(
        grad_halos, neighbour_code[own_index], neighbour_shift[own_index]
    ).astype(jnp.bfloat16)
    arrived = nearby_adjoints(returned.reshape(1, 4, 3, tile_side * channels))
    senders = (own_index + jnp.arange(2 * REACH + 1, dtype=jnp.int32) - REACH) % tiles
    hitting = (senders[:, None] + neighbour_step[senders]) % tiles == own_index
    targets = neighbour_code[senders] // 2
    selector = hitting[None] & (targets[None] == jnp.arange(4, dtype=jnp.int32)[:, None, None])
    selector = selector.astype(jnp.bfloat16).reshape(4, (2 * REACH + 1) * 4)
    grad_bands = jnp.dot(
        selector, arrived.reshape((2 * REACH + 1) * 4, -1), preferred_element_type=jnp.float32
    )
    grad_bands = grad_bands.reshape(4, 3, tile_side, channels)
    d_field = (
        grad_out
        + grad_ext[3 : tile_side + 3, 3 : tile_side + 3]
        + band_adjoint(grad_bands, tile_len)
    )
    input_grad = jnp.where(inside, d_field, 0.0).astype(jnp.bfloat16)
    scale = 1.0 / math.sqrt(samples * tiles * tile_side * tile_side)
    local_grads = jnp.concatenate([grad_in.reshape(-1), grad_proj.reshape(-1)]) * scale
    partial_grads = lax.psum_scatter(
        local_grads.astype(jnp.bfloat16), "dp", scatter_dimension=0, tiled=True
    ).astype(jnp.float32)
    weight_grads = lax.psum_scatter(partial_grads, "space", scatter_dimension=0, tiled=True)
    return (
        outputs.astype(jnp.bfloat16).reshape(1, 1, tile_side, tile_side * channels),
        input_grad.reshape(1, 1, tile_side, tile_side * channels),
        weight_grads,
    )


def solution(mesh):
    placed = (
        P("dp", "space", None, None),
        P("dp", "space", None, None),
        P(),
        P(),
        P(),
        P(),
        P(),
        P(),
        P(),
        P(),
        P(),
        P(),
        P(),
        P(),
        P(),
    )
    return jax.shard_map(
        local,
        mesh=mesh,
        in_specs=placed,
        out_specs=(P("dp", "space", None, None), P("dp", "space", None, None), P(("dp", "space"))),
        check_vma=False,
    )
```

profile of v0, /device:TPU:2, one launch (start us, length us, event | category | flops | bytes accessed | tf_op | source)
XLA Modules:
  0.0 778.6 jit_solution(9950928501189964560)
XLA Ops:
  7.3 1.3 dynamic_slice.76
  8.6 0.6 iota_compare_fusion.1
  9.3 1.2 reshape_squeeze.4
  12.6 0.8 compare_and_fusion
  13.6 3.8 collective-permute-start
  17.4 19.4 %collective-permute-start.1 = (bf16[1,4,3,4608]{3,2,1,0:T(4,128)(2,1)S(1)}, bf16[1,4,3,4608]{3,2,1,0:T(4,128)(2,1)S(1)}, u32[]{:S(2)}, u32[]{:S(2)}) collective-permute-start(bf16[1,4,3,4608]{3,2,1,0:T(4,128)(2,1)S(1)} %pad_maximum_fusion.3), channel_id=1, source_target_pairs={{0,63},{1,0},{2,1},{3,2},{4,3},{5,4},{6,5},{7,6},{8,7},{9,8},{10,9... | collective-permute-start | bytes 331784 | tf_op jit(solution)/shard_map/ppermute | solution.py:17
  47.5 0.7 constant_dynamic-slice_fusion.14
  61.0 1.3 dynamic-slice.62
  62.3 1.3 dynamic-slice.64
  68.8 2.0 fusion.33
  70.8 1.5 scatter.15
  73.4 3.1 fusion.9
  77.5 1.6 multiply_convert_fusion
  79.2 1.3 fusion.4
  80.4 1.3 fusion.51
  83.2 3.1 fusion.67
  86.3 6.9 fusion.16
  94.4 0.7 gather_fusion.3
  95.7 1.9 collective-permute-start.2
  97.6 7.7 collective-permute-start.3
  105.4 2.9 fusion.50
  108.3 1.5 reshape.624
  109.8 0.9 fusion.8
  110.8 1.7 fusion.6
  113.0 0.8 select_convert_fusion
  113.8 1.2 pad_maximum_fusion.1
  116.7 0.7 scatter_fusion
  118.4 131.1 %all-reduce.12.cloned.1.call-done = bf16[294912]{0:T(1024)(128)(2,1)} async-done(((bf16[294912]{0:T(1024)(128)(2,1)}), bf16[294912]{0:T(1024)(128)(2,1)}) %all-reduce.12.cloned.1.call-update) | async-done | bytes 589840
  249.4 1.4 dynamic-slice_convert_fusion
  251.0 0.9 reshape.622
  252.0 518.4 %all-reduce.14.cloned.1.call-done = f32[18432]{0:T(1024)} async-done(((f32[18432]{0:T(1024)}), f32[18432]{0:T(1024)}) %all-reduce.14.cloned.1.call-update) | async-done | bytes 73744
  770.4 1.3 dynamic-slice.65
  (161 shorter events, 15.1 us)
Async XLA Ops:
  7.2 70.3 %copy-start = (bf16[192,768]{1,0:T(8,128)(2,1)S(1)}, bf16[192,768]{1,0:T(8,128)(2,1)}, u32[]{:S(2)}) copy-start(bf16[192,768]{1,0:T(8,128)(2,1)} %param.39) | copy-start | bytes 884740
  7.2 5.4 copy-start.14
  7.2 29.7 %copy-start.7 = (s32[64,4]{0,1:T(4,128)S(1)}, s32[64,4]{0,1:T(4,128)}, u32[]{:S(2)}) copy-start(s32[64,4]{0,1:T(4,128)} %param.33) | copy-start | bytes 3076
  7.2 40.3 %copy-start.10 = (s32[64,4]{0,1:T(4,128)S(1)}, s32[64,4]{0,1:T(4,128)}, u32[]{:S(2)}) copy-start(s32[64,4]{0,1:T(4,128)} %param.32) | copy-start | bytes 3076
  7.2 40.3 %copy-start.9 = (s32[64,4]{0,1:T(4,128)S(1)}, s32[64,4]{0,1:T(4,128)}, u32[]{:S(2)}) copy-start(s32[64,4]{0,1:T(4,128)} %param.34) | copy-start | bytes 3076
  7.2 51.8 %copy-start.2 = (bf16[1,1,24,4608]{3,2,1,0:T(8,128)(2,1)S(1)}, bf16[1,1,24,4608]{3,2,1,0:T(8,128)(2,1)}, u32[]{:S(2)}) copy-start(bf16[1,1,24,4608]{3,2,1,0:T(8,128)(2,1)} %param.30) | copy-start | bytes 663556
  7.2 242.2 %all-reduce.12.cloned.1.call-start = ((), (), s32[]{:S(2)}) async-start(), calls=%async_computation | async-start | bytes 1179648
  12.2 52.9 %copy-start.12 = (f32[192]{0:T(256)S(1)}, f32[192]{0:T(256)}, u32[]{:S(2)}) copy-start(f32[192]{0:T(256)} %param.43) | copy-start | bytes 2308
  13.6 53.5 %collective-permute-start = (bf16[1,4,3,4608]{3,2,1,0:T(4,128)(2,1)S(1)}, bf16[1,4,3,4608]{3,2,1,0:T(4,128)(2,1)S(1)}, u32[]{:S(2)}, u32[]{:S(2)}) collective-permute-start(bf16[1,4,3,4608]{3,2,1,0:T(4,128)(2,1)S(1)} %pad_maximum_fusion.3), channel_id=1, source_target_pairs={{0,1},{1,2},{2,3},{3,4},{4,5},{5,6},{6,7},{7,8},{8,9},{9,10},{10,1... | collective-permute-start | bytes 331784 | tf_op jit(solution)/shard_map/ppermute | solution.py:17
  17.4 49.7 %collective-permute-start.1 = (bf16[1,4,3,4608]{3,2,1,0:T(4,128)(2,1)S(1)}, bf16[1,4,3,4608]{3,2,1,0:T(4,128)(2,1)S(1)}, u32[]{:S(2)}, u32[]{:S(2)}) collective-permute-start(bf16[1,4,3,4608]{3,2,1,0:T(4,128)(2,1)S(1)} %pad_maximum_fusion.3), channel_id=1, source_target_pairs={{0,63},{1,0},{2,1},{3,2},{4,3},{5,4},{6,5},{7,6},{8,7},{9,8},{10,9... | collective-permute-start | bytes 331784 | tf_op jit(solution)/shard_map/ppermute | solution.py:17
  59.2 19.9 %copy-start.4 = (f32[576,192]{1,0:T(8,128)}, f32[576,192]{1,0:T(8,128)S(1)}, u32[]{:S(2)}) copy-start(f32[576,192]{1,0:T(8,128)S(1)} %reshape.627) | copy-start | bytes 1327108
  67.5 5.9 copy-start.15
  73.4 3.2 copy-start.6
  76.5 1.0 copy-start.8
  76.5 1.0 copy-start.11
  76.5 1.0 copy-start.17
  77.5 1.7 copy-start.5
  82.4 3.8 copy-start.16
  93.7 11.7 %copy-start.1 = (f32[192,768]{1,0:T(8,128)S(1)}, f32[192,768]{1,0:T(8,128)}, u32[]{:S(2)}) copy-start(f32[192,768]{1,0:T(8,128)} %fusion.51) | copy-start | bytes 1769476
  95.7 18.2 %collective-permute-start.2 = (bf16[1,4,3,4608]{3,1,2,0:T(4,128)(2,1)S(1)}, bf16[1,4,3,4608]{3,1,2,0:T(4,128)(2,1)}, u32[]{:S(2)}, u32[]{:S(2)}) collective-permute-start(bf16[1,4,3,4608]{3,1,2,0:T(4,128)(2,1)S(1)} %copy.124), channel_id=1, source_target_pairs={{0,1},{1,2},{2,3},{3,4},{4,5},{5,6},{6,7},{7,8},{8,9},{9,10},{10,1... | collective-permute-start | bytes 331784 | tf_op jit(solution)/shard_map/ppermute | solution.py:17
  97.6 16.2 %collective-permute-start.3 = (bf16[1,4,3,4608]{3,1,2,0:T(4,128)(2,1)S(1)}, bf16[1,4,3,4608]{3,1,2,0:T(4,128)(2,1)}, u32[]{:S(2)}, u32[]{:S(2)}) collective-permute-start(bf16[1,4,3,4608]{3,1,2,0:T(4,128)(2,1)S(1)} %copy.124), channel_id=1, source_target_pairs={{0,63},{1,0},{2,1},{3,2},{4,3},{5,4},{6,5},{7,6},{8,7},{9,8},{10,9... | collective-permute-start | bytes 331784 | tf_op jit(solution)/shard_map/ppermute | solution.py:17
  108.3 2.6 copy-start.13
  110.8 2.2 copy-start.3
  110.8 659.6 %all-reduce.14.cloned.1.call-start = ((), (), s32[]{:S(2)}) async-start(), calls=%async_computation.1 | async-start | bytes 147456
Sparse Core Ops, SparseCore 0:
  110.9 138.4 all-reduce.11
  253.3 517.0 all-reduce.13
where the time goes:
time: 779 us
  waiting for transfers between devices  649 us (83%)
  between operations  38.7 us (5%)
  starting transfers between devices  32.9 us (4%)
  local copies, waits for them, and re-layouts  23.5 us (3%)
  matrix products  19.5 us (3%)
  other arithmetic  14.4 us (2%)
    unnamed x4, waiting for transfers between devices  649 us
    ppermute x4, starting transfers between devices, from_behind(): lax.ppermute(array, axis, [(i, (i + by) % length) for i in range(length)])  32.9 us
  transfers between devices with their start and end apart: 6, of which 2 were waited for; matrix products, arithmetic and copies ran while one was open for 3% of the time, Pallas kernels for 0%

commit v1 on v0

v1 whole, which is shorter than its diff:
```python
import math

import jax
import jax.numpy as jnp
from jax import lax
from jax.experimental import pallas as pl
from jax.experimental.pallas import tpu as pltpu
from jax.sharding import PartitionSpec as P

C = 192
H = 768
TS = 24
CELLS = TS * TS
TILES = 64
SAMPLES = 16
WIDE = TS * C
PAIR = 2 * C
ROOT_HALF = 0.7071067811865476
INV_ROOT_TAU = 0.3989422804014327
SCALE = 1.0 / math.sqrt(SAMPLES * TILES * CELLS)
F32 = jnp.float32
BF16 = jnp.bfloat16
MESH = pl.DeviceIdType.MESH
SMEM = pl.BlockSpec(memory_space=pltpu.SMEM)
VMEM = pl.BlockSpec(memory_space=pltpu.VMEM)


def iota(shape, dim):
    return lax.broadcasted_iota(jnp.int32, shape, dim)


def one_hot(found, wanted):
    return jnp.where(found == wanted, 1.0, 0.0).astype(BF16)


def dot(a, b):
    return jnp.dot(a, b, preferred_element_type=F32)


def dot_tb(a, b):
    return lax.dot_general(a, b, (((1,), (1,)), ((), ())), preferred_element_type=F32)


def dot_ta(a, b):
    return lax.dot_general(a, b, (((0,), (0,)), ((), ())), preferred_element_type=F32)


def columns_of(ref):
    columns = []
    for p in range(TS // 2):
        pair = ref[:, p * PAIR : (p + 1) * PAIR].astype(F32)
        columns += [pair[:, :C], pair[:, C:]]
    return columns


def band_cells(tile_len):
    i = iota((TS, 1), 0)
    parts = []
    for k in range(3):
        parts.append(i * TS + k)
        parts.append(i * TS + (tile_len - 1 - k))
        parts.append(jnp.where(i < tile_len, k * TS + i, -1))
        parts.append(jnp.where(i < tile_len, (TS - 1 - k) * TS + i, -1))
    return parts


def oriented(position, code, shift):
    unshifted = position - shift
    index = jnp.where(code % 2 == 1, TS - 1 - unshifted, unshifted)
    return index, (unshifted >= 0) & (unshifted < TS)


def bands_kernel(
    rows_ref, step_ref, code_ref, shift_ref, x_ref, halo_ref, own, from_lo, from_hi, send, recv
):
    me = lax.axis_index("space")
    dp = lax.axis_index("dp")
    hi = lax.rem(me + 1, TILES)
    lo = lax.rem(me + TILES - 1, TILES)
    barrier = pltpu.get_barrier_semaphore()
    for peer in (lo, hi):
        pl.semaphore_signal(barrier, inc=1, device_id=(dp, peer), device_id_type=MESH)
    cells = jnp.concatenate(columns_of(x_ref), axis=0).astype(BF16)
    wanted = jnp.concatenate(band_cells(rows_ref[me]), axis=0)
    own[...] = dot(one_hot(iota((288, CELLS), 1), wanted), cells).astype(BF16)
    pl.semaphore_wait(barrier, 2)
    copies = []
    for n, (peer, landing) in enumerate(((hi, from_lo), (lo, from_hi))):
        copy = pltpu.make_async_remote_copy(
            src_ref=own,
            dst_ref=landing,
            send_sem=send.at[n],
            recv_sem=recv.at[n],
            device_id=(dp, peer),
            device_id_type=MESH,
        )
        copy.start()
        copies.append(copy)
    position = iota((TS, 1), 0)
    picks = []
    for source in range(3):
        parts = []
        for q in range(4):
            code = code_ref[q, me]
            index, on_band = oriented(position, code, shift_ref[q, me])
            first = jnp.where(step_ref[q, me] + 1 == source, (code // 2) * TS, -1000)
            parts.append(jnp.where(on_band, first + index, -1))
        picks.append(one_hot(iota((96, 96), 1), jnp.concatenate(parts, axis=0)))
    for copy in copies:
        copy.wait()
    for k in range(3):
        rows = slice(96 * k, 96 * k + 96)
        halo_ref[rows, :] = (
            dot(picks[0], from_lo[rows, :])
            + dot(picks[1], own[rows, :])
            + dot(picks[2], from_hi[rows, :])
        ).astype(BF16)


def block_kernel(
    rows_ref,
    x_ref,
    c_ref,
    halo_ref,
    kern_ref,
    bias_ref,
    gain_ref,
    shift_ref,
    we_ref,
    be_ref,
    wp_ref,
    bp_ref,
    ls_ref,
    out_ref,
    base_ref,
    dh_ref,
    gi_ref,
    gp_ref,
    weights,
    ext,
    ext_at,
    mixed,
    normal,
    rstd,
    normed,
    d_branch,
    branch,
    d_normed,
    d_pad,
    d_at,
    d_ext,
):
    tile_len = rows_ref[lax.axis_index("space")]
    inside = iota((TS, C), 0) < tile_len
    for t in range(49):
        weights[t] = jnp.broadcast_to(kern_ref[t : t + 1, :], (8, C))

    halo = halo_ref[...].astype(F32)
    col = iota((1, 144), 1)
    target = col
    for m in range(6):
        row = (7 - m // 2) if m % 2 == 0 else (tile_len + 8 + m // 2)
        target = jnp.where(col >= TS * m, col * 40 + (row - 960 * m), target)
    edge_rows = jnp.concatenate([halo[96 * k : 96 * k + 48] for k in range(3)], axis=0).astype(BF16)
    ext[3:27] = dot(one_hot(iota((960, 144), 0), target), edge_rows).reshape(TS, 40, C)
    blank = jnp.zeros((40, C), F32)
    for k in range(3):
        ext[2 - k] = blank
        ext[27 + k] = blank
        ext[2 - k, 8:32] = halo[96 * k + 48 : 96 * k + 72]
        ext[27 + k, 8:32] = halo[96 * k + 72 : 96 * k + 96]
    for j, column in enumerate(columns_of(x_ref)):
        ext[3 + j, 8:32] += jnp.where(inside, column, 0.0)

    @pl.loop(0, 30)
    def _(at):
        whole = ext[at]
        for a in range(7):
            ext_at[a, at] = whole[5 + a : 29 + a]

    @pl.loop(0, 6)
    def _(block):
        first = block * 4
        totals = [jnp.broadcast_to(bias_ref[...], (TS, C)) for _ in range(4)]
        for a in range(7):
            for column in range(10):
                value = ext_at[a, first + column].reshape(3, 8, C)
                for j in range(4):
                    b = column - j
                    if 0 <= b < 7:
                        totals[j] = totals[j] + (value * weights[7 * a + b][None]).reshape(TS, C)
        for j in range(4):
            mixed[pl.ds((first + j) * TS, TS), :] = totals[j]

    @pl.loop(0, 6)
    def _(block):
        rows = pl.ds(pl.multiple_of(block * 96, 96), 96)
        value = mixed[rows, :]
        centred = value - jnp.mean(value, axis=1, keepdims=True)
        inverse = lax.rsqrt(jnp.mean(centred * centred, axis=1, keepdims=True) + 1e-06)
        scaled = centred * inverse
        normal[rows, :] = scaled
        rstd[rows, :] = jnp.broadcast_to(inverse, (96, 128))
        normed[rows, :] = (scaled * gain_ref[...] + shift_ref[...]).astype(BF16)

    grads = [jnp.where(inside, column, 0.0) for column in columns_of(c_ref)]
    for j in range(TS):
        base_ref[j * TS : j * TS + TS, :] = grads[j]
    d_branch[...] = (base_ref[...] * ls_ref[...]).astype(BF16)

    grad_in, grad_proj = [], []
    for chunk in range(3):
        hidden = slice(256 * chunk, 256 * chunk + 256)
        pre = dot(normed[...], we_ref[:, hidden]) + be_ref[:, hidden]
        phi = 0.5 * (1.0 + lax.erf(pre * ROOT_HALF))
        act = (pre * phi).astype(BF16)
        slope = phi + pre * INV_ROOT_TAU * jnp.exp(-0.5 * pre * pre)
        d_act = dot_tb(d_branch[...], wp_ref[hidden, :])
        d_pre = (d_act * slope).astype(BF16)
        forward = dot(act, wp_ref[hidden, :])
        backward = dot_tb(d_pre, we_ref[:, hidden])
        if chunk == 0:
            branch[...] = forward
            d_normed[...] = backward
        else:
            branch[...] += forward
            d_normed[...] += backward
        grad_in.append(dot_ta(normed[...], d_pre) * SCALE)
        grad_proj.append(dot_ta(act, d_branch[...]) * SCALE)
    grad_in = jnp.concatenate(grad_in, axis=1)
    grad_proj = jnp.concatenate(grad_proj, axis=0)
    for core in range(2):
        for x in range(2):
            gi_ref[core, x] = jnp.concatenate(
                [grad_in[24 * d : 24 * d + 24] for d in (4 * x + core, 4 * x + 2 + core)], axis=0
            ).astype(BF16)
            gp_ref[core, x] = jnp.concatenate(
                [grad_proj[96 * d : 96 * d + 96] for d in (4 * x + core, 4 * x + 2 + core)], axis=1
            ).astype(BF16)

    for p, (left, right) in enumerate(zip(*[iter(columns_of(x_ref))] * 2)):
        pair = []
        for j, column in ((2 * p, left), (2 * p + 1, right)):
            value = (branch[j * TS : j * TS + TS, :] + bp_ref[...]).astype(BF16).astype(F32)
            pair.append(jnp.where(inside, column + ls_ref[...] * value, 0.0))
        out_ref[:, p * PAIR : (p + 1) * PAIR] = jnp.concatenate(pair, axis=1).astype(BF16)

    d_pad[...] = jnp.zeros_like(d_pad)

    @pl.loop(0, 6)
    def _(block):
        rows = pl.ds(pl.multiple_of(block * 96, 96), 96)
        grad = d_normed[rows, :].astype(BF16).astype(F32) * gain_ref[...]
        scaled = normal[rows, :]
        mean = jnp.mean(grad, axis=1, keepdims=True)
        along = jnp.mean(grad * scaled, axis=1, keepdims=True)
        value = rstd[rows, 0:1] * (grad - mean - scaled * along)
        for j in range(4):
            d_pad[block * 4 + j + 6, 8:32] = value[j * TS : j * TS + TS]

    @pl.loop(0, 36)
    def _(at):
        whole = d_pad[at]
        for a in range(7):
            d_at[a, at] = whole[8 - a : 40 - a]

    @pl.loop(0, 10)
    def _(block):
        first = block * 3
        totals = [jnp.zeros((32, C), F32) for _ in range(3)]
        for a in range(7):
            for column in range(9):
                value = d_at[a, first + column].reshape(4, 8, C)
                for j in range(3):
                    b = j - column + 6
                    if 0 <= b < 7:
                        totals[j] = totals[j] + (value * weights[7 * a + b][None]).reshape(32, C)
        for j in range(3):
            d_ext[first + j] = totals[j]

    parts = []
    j = iota((TS, 1), 0)
    for m in range(6):
        parts.append(j * 32 + ((2 - m // 2) if m % 2 == 0 else (tile_len + 3 + m // 2)))
    middle = d_ext[3:27].reshape(TS * 32, C).astype(BF16)
    edge_rows = dot(one_hot(iota((144, TS * 32), 1), jnp.concatenate(parts, axis=0)), middle)
    parts = []
    for k in range(3):
        parts += [
            edge_rows[48 * k : 48 * k + 48],
            d_ext[2 - k, 3:27],
            d_ext[27 + k, 3:27],
        ]
    dh_ref[...] = jnp.concatenate(parts, axis=0).astype(BF16)
    for j in range(TS):
        base_ref[j * TS : j * TS + TS, :] += d_ext[3 + j, 3:27]


def finish_kernel(
    rows_ref,
    step_ref,
    code_ref,
    shift_ref,
    gi_ref,
    gp_ref,
    dh_ref,
    base_ref,
    ig_ref,
    wg_ref,
    dh_lo,
    dh_hi,
    core_i,
    core_p,
    xs_i,
    xs_p,
    xr_i,
    xr_p,
    ys_i,
    ys_p,
    yr_i,
    yr_p,
    hs_i,
    hs_p,
    hr_i,
    hr_p,
    ls_i,
    ls_p,
    lr_i,
    lr_p,
    own_x_i,
    own_x_p,
    own_y_i,
    own_y_p,
    own_h_i,
    own_h_p,
    dh_send,
    dh_recv,
    core_send,
    core_recv,
    x_send,
    x_recv,
    y_send,
    y_recv,
    h_send,
    h_recv,
    l_send,
    l_recv,
):
    me = lax.axis_index("space")
    dp = lax.axis_index("dp")
    mx = dp // 4
    core = lax.rem(dp, 2)
    my = (me // 32) * 2 + lax.rem(dp // 2, 2)
    z = lax.rem(me, 32)
    mh = z // 8
    ml = lax.rem(z, 8)
    hi = lax.rem(me + 1, TILES)
    lo = lax.rem(me + TILES - 1, TILES)
    other = dp + 1 - 2 * core

    def at_x(x):
        return (x * 4 + lax.rem(dp, 4), me)

    def at_y(y):
        return (mx * 4 + lax.rem(y, 2) * 2 + core, (y // 2) * 32 + z)

    def at_h(h):
        return (dp, (me // 32) * 32 + h * 8 + ml)

    def at_l(lane):
        return (dp, (me // 8) * 8 + lane)

    xs = [lax.rem(mx + d, 4) for d in (1, 2, 3)]
    ys = [lax.rem(my + d, 4) for d in (1, 2, 3)]
    hs = [lax.rem(mh + d, 4) for d in (1, 2, 3)]
    lanes = [lax.rem(ml + d, 8) for d in range(1, 8)]
    peers = [(dp, lo), (dp, hi), (other, me)]
    peers += [at_x(x) for x in xs] + [at_y(y) for y in ys]
    peers += [at_h(h) for h in hs] + [at_l(lane) for lane in lanes]
    barrier = pltpu.get_barrier_semaphore()
    for peer in peers:
        pl.semaphore_signal(barrier, inc=1, device_id=peer, device_id_type=MESH)
    pl.semaphore_wait(barrier, len(peers))

    def remote(source, landing, send, recv, peer):
        return pltpu.make_async_remote_copy(
            src_ref=source,
            dst_ref=landing,
            send_sem=send,
            recv_sem=recv,
            device_id=peer,
            device_id_type=MESH,
        )

    core_copies = [
        remote(gi_ref.at[1 - core], core_i, core_send.at[0], core_recv.at[0], (other, me)),
        remote(gp_ref.at[1 - core], core_p, core_send.at[1], core_recv.at[1], (other, me)),
    ]
    dh_copies = [
        remote(dh_ref, dh_lo, dh_send.at[0], dh_recv.at[0], (dp, hi)),
        remote(dh_ref, dh_hi, dh_send.at[1], dh_recv.at[1], (dp, lo)),
    ]
    for copy in core_copies + dh_copies:
        copy.start()
    for copy in core_copies:
        copy.wait()
    for x in range(2):
        sum_i = gi_ref[core, x].astype(F32) + core_i[x].astype(F32)
        sum_p = gp_ref[core, x].astype(F32) + core_p[x].astype(F32)
        own_x_i[x] = sum_i
        own_x_p[x] = sum_p
        xs_i[x] = sum_i.astype(BF16)
        xs_p[x] = sum_p.astype(BF16)

    def x_copy(n, x, wide):
        if wide:
            return remote(xs_i.at[x], xr_i.at[n], x_send.at[n], x_recv.at[n], at_x(x))
        return remote(xs_p.at[x - 2], xr_p.at[n], x_send.at[n], x_recv.at[n], at_x(x))

    for n, x in enumerate(xs):

        @pl.when(x < 2)
        def _():
            x_copy(n, x, True).start()

        @pl.when(x >= 2)
        def _():
            x_copy(n, x, False).start()

    tile_len = rows_ref[me]
    spread = []
    lane = iota((1, 96), 1)
    for source in range(3):
        sender = lax.rem(me + source + TILES - 1, TILES)
        target = jnp.full((1, 96), -1, jnp.int32)
        for q in range(4):
            code = code_ref[q, sender]
            index, on_band = oriented(lane - TS * q, code, shift_ref[q, sender])
            first = jnp.where(step_ref[q, sender] == 1 - source, (code // 2) * TS, -1000)
            mine = (lane >= TS * q) & (lane < TS * q + TS)
            target = jnp.where(mine & on_band, first + index, target)
        spread.append(one_hot(iota((96, 96), 0), target))
    cell = jnp.concatenate(band_cells(tile_len), axis=0)
    to_bands = one_hot(iota((288, CELLS), 1), cell)
    for copy in dh_copies:
        copy.wait()
    parts = []
    for k in range(3):
        rows = slice(96 * k, 96 * k + 96)
        parts.append(
            dot(spread[0], dh_lo[rows, :])
            + dot(spread[1], dh_ref[rows, :])
            + dot(spread[2], dh_hi[rows, :])
        )
    d_bands = jnp.concatenate(parts, axis=0)
    upper = d_bands.astype(BF16)
    lower = (d_bands - upper.astype(F32)).astype(BF16)
    total = base_ref[...] + (dot_ta(to_bands, upper) + dot_ta(to_bands, lower))
    inside = iota((TS, PAIR), 0) < tile_len
    for p in range(TS // 2):
        pair = [total[j * TS : j * TS + TS] for j in (2 * p, 2 * p + 1)]
        ig_ref[:, p * PAIR : (p + 1) * PAIR] = jnp.where(
            inside, jnp.concatenate(pair, axis=1), 0.0
        ).astype(BF16)

    def exchange(peers_at, send_refs, recv_ref, send, recv):
        copies = []
        for n, (source, device) in enumerate(zip(send_refs, peers_at)):
            copies.append(remote(source, recv_ref.at[n], send.at[n], recv.at[n], device))
        for copy in copies:
            copy.start()
        for copy in copies:
            copy.wait()

    def tail(wide, own_x, xr, own_y, ysend, yr, own_h, hsend, hr, lsend, lr):
        total = own_x[mx if wide else mx - 2]
        for n in range(3):
            total = total + xr[n].astype(F32)
        count = 12 if wide else 48
        for y in range(4):
            if wide:
                part = total[24 * (y % 2) + 12 * (y // 2) :][:12]
            else:
                part = total[48 * (y // 2) :][:48, C * (y % 2) :][:, :C]
            own_y[y, 0:count] = part
            ysend[y, 0:count] = part.astype(BF16)
        exchange([at_y(y) for y in ys], [ysend.at[y] for y in ys], yr, y_send, y_recv)
        total = own_y[my, 0:count]
        for n in range(3):
            total = total + yr[n, 0:count].astype(F32)
        count = count // 4
        for h in range(4):
            part = total[h * count : h * count + count]
            own_h[h, 0:count] = part
            hsend[h, 0:count] = part.astype(BF16)
        exchange([at_h(h) for h in hs], [hsend.at[h] for h in hs], hr, h_send, h_recv)
        total = own_h[mh, 0:count]
        for n in range(3):
            total = total + hr[n, 0:count].astype(F32)
        lsend[0:count] = total.astype(BF16)
        exchange([at_l(lane) for lane in lanes], [lsend] * 7, lr, l_send, l_recv)
        for n in range(7):
            total = total + lr[n, 0:count].astype(F32)
        width = total.shape[1]
        for m in range(8):
            pieces, at = [], 288 * m
            while at < 288 * m + 288:
                row, first = at // width, at % width
                size = min(288 * m + 288 - at, width - first)
                pieces.append(total[row : row + 1, first : first + size])
                at += size

            @pl.when(ml == m)
            def _():
                wg_ref[...] = jnp.concatenate(pieces, axis=1) if len(pieces) > 1 else pieces[0]

    @pl.when(mx < 2)
    def _():
        for n, x in enumerate(xs):
            remote(xs_i.at[0], xr_i.at[n], x_send.at[n], x_recv.at[n], at_x(x)).wait_recv()
        tail(True, own_x_i, xr_i, own_y_i, ys_i, yr_i, own_h_i, hs_i, hr_i, ls_i, lr_i)

    @pl.when(mx >= 2)
    def _():
        for n, x in enumerate(xs):
            remote(xs_p.at[0], xr_p.at[n], x_send.at[n], x_recv.at[n], at_x(x)).wait_recv()
        tail(False, own_x_p, xr_p, own_y_p, ys_p, yr_p, own_h_p, hs_p, hr_p, ls_p, lr_p)

    for n, x in enumerate(xs):

        @pl.when(x < 2)
        def _():
            x_copy(n, x, True).wait_send()

        @pl.when(x >= 2)
        def _():
            x_copy(n, x, False).wait_send()


def local(
    inputs,
    cotangent,
    tile_rows,
    neighbour_step,
    neighbour_code,
    neighbour_shift,
    conv_kernel,
    conv_bias,
    norm_gain,
    norm_bias,
    w_expand,
    b_expand,
    w_project,
    b_project,
    layer_scale,
):
    x = inputs.reshape(TS, WIDE)
    c = cotangent.reshape(TS, WIDE)
    tables = (neighbour_step.T, neighbour_code.T, neighbour_shift.T)
    dma = pltpu.SemaphoreType.DMA
    halo = pl.pallas_call(
        bands_kernel,
        out_shape=jax.ShapeDtypeStruct((288, C), BF16),
        in_specs=[SMEM] * 4 + [VMEM],
        out_specs=VMEM,
        scratch_shapes=[pltpu.VMEM((288, C), BF16)] * 3 + [dma((2,)), dma((2,))],
        compiler_params=pltpu.CompilerParams(
            collective_id=0, has_side_effects=True, vmem_limit_bytes=16 << 20
        ),
        name="bands",
    )(tile_rows, *tables, x)
    out, base, dh, gi, gp = pl.pallas_call(
        block_kernel,
        out_shape=(
            jax.ShapeDtypeStruct((TS, WIDE), BF16),
            jax.ShapeDtypeStruct((CELLS, C), F32),
            jax.ShapeDtypeStruct((288, C), BF16),
            jax.ShapeDtypeStruct((2, 2, 48, H), BF16),
            jax.ShapeDtypeStruct((2, 2, 96, PAIR), BF16),
        ),
        in_specs=[SMEM] + [VMEM] * 12,
        out_specs=(VMEM,) * 5,
        scratch_shapes=[
            pltpu.VMEM((49, 8, C), F32),
            pltpu.VMEM((30, 40, C), F32),
            pltpu.VMEM((7, 30, TS, C), F32),
            pltpu.VMEM((CELLS, C), F32),
            pltpu.VMEM((CELLS, C), F32),
            pltpu.VMEM((CELLS, 128), F32),
            pltpu.VMEM((CELLS, C), BF16),
            pltpu.VMEM((CELLS, C), BF16),
            pltpu.VMEM((CELLS, C), F32),
            pltpu.VMEM((CELLS, C), F32),
            pltpu.VMEM((36, 40, C), F32),
            pltpu.VMEM((7, 36, 32, C), F32),
            pltpu.VMEM((30, 32, C), F32),
        ],
        compiler_params=pltpu.CompilerParams(vmem_limit_bytes=48 << 20),
        name="block",
    )(
        tile_rows,
        x,
        c,
        halo,
        conv_kernel.reshape(49, C),
        conv_bias.reshape(1, C),
        norm_gain.reshape(1, C),
        norm_bias.reshape(1, C),
        w_expand,
        b_expand.reshape(1, H),
        w_project,
        b_project.reshape(1, C),
        layer_scale.reshape(1, C),
    )
    vm = pltpu.VMEM
    ig, wg = pl.pallas_call(
        finish_kernel,
        out_shape=(
            jax.ShapeDtypeStruct((TS, WIDE), BF16),
            jax.ShapeDtypeStruct((1, 288), F32),
        ),
        in_specs=[SMEM] * 4 + [VMEM] * 4,
        out_specs=(VMEM, VMEM),
        scratch_shapes=[
            vm((288, C), BF16),
            vm((288, C), BF16),
            vm((2, 48, H), BF16),
            vm((2, 96, PAIR), BF16),
            vm((2, 48, H), BF16),
            vm((2, 96, PAIR), BF16),
            vm((3, 48, H), BF16),
            vm((3, 96, PAIR), BF16),
            vm((4, 16, H), BF16),
            vm((4, 48, C), BF16),
            vm((3, 16, H), BF16),
            vm((3, 48, C), BF16),
            vm((4, 16, H), BF16),
            vm((4, 16, C), BF16),
            vm((3, 16, H), BF16),
            vm((3, 16, C), BF16),
            vm((16, H), BF16),
            vm((16, C), BF16),
            vm((7, 16, H), BF16),
            vm((7, 16, C), BF16),
            vm((2, 48, H), F32),
            vm((2, 96, PAIR), F32),
            vm((4, 16, H), F32),
            vm((4, 48, C), F32),
            vm((4, 16, H), F32),
            vm((4, 16, C), F32),
        ]
        + [dma((2,))] * 4
        + [dma((3,))] * 6
        + [dma((7,))] * 2,
        compiler_params=pltpu.CompilerParams(
            collective_id=1, has_side_effects=True, vmem_limit_bytes=32 << 20
        ),
        name="finish",
    )(tile_rows, *tables, gi, gp, dh, base)
    return (
        out.reshape(1, 1, TS, WIDE),
        ig.reshape(1, 1, TS, WIDE),
        wg.reshape(288),
    )


def solution(mesh):
    field = P("dp", "space", None, None)
    return jax.shard_map(
        local,
        mesh=mesh,
        in_specs=(field, field) + (P(),) * 13,
        out_specs=(field, field, P(("dp", "space"))),
        check_vma=False,
    )
```

time: 779 us -> 91.4 us (0.12)
  the two profiles are of different devices: /device:TPU:2 before, /device:TPU:1 now
where the time goes in v1:
time: 91.4 us; the launch traced here: 91.1 us
  Pallas kernels  85.3 us (93%)
  local copies, waits for them, and re-layouts  4.44 us (5%)
    pallas_call x1, Pallas kernels, local(): pl.pallas_call(finish_kernel, out_shape=(jax.ShapeDtypeStruct((TS, WIDE),...  44.4 us
    pallas_call x1, Pallas kernels, local(): pl.pallas_call(bands_kernel, out_shape=jax.ShapeDtypeStruct((288, C), BF1...  25.8 us
    pallas_call x1, Pallas kernels, local(): pl.pallas_call(block_kernel, out_shape=(jax.ShapeDtypeStruct((TS, WIDE),...  15 us
    unnamed x30, local copies, waits for them, and re-layouts  3.57 us

profile of v1, /device:TPU:1, one launch (start us, length us, event | category | flops | bytes accessed | tf_op | source)
XLA Modules:
  0.0 91.1 jit_solution(12234335156246328732)
XLA Ops:
  0.6 0.0 copy-start.13
  0.6 0.7 copy-done.13
  1.3 0.0 copy-start.4
  1.3 0.0 copy-start.7
  1.3 0.9 reshape.44.kern_ref
  2.2 0.0 copy-done.4
  2.2 0.0 copy-done.5
  2.2 0.0 copy-done.6
  2.2 0.0 copy-done.7
  2.2 0.0 copy-start
  2.3 0.9 %copy-done = bf16[1,1,24,4608]{3,2,1,0:T(8,128)(2,1)S(1)} copy-done((bf16[1,1,24,4608]{3,2,1,0:T(8,128)(2,1)S(1)}, bf16[1,1,24,4608]{3,2,1,0:T(8,128)(2,1)}, u32[]{:S(2)}) %copy-start) | copy-done | bytes 221208
  3.2 25.8 %bands.1.halo_ref = bf16[288,192]{1,0:T(8,128)(2,1)S(1)} custom-call(s32[64]{0:T(128)S(1)} %copy-done.7, s32[4,64]{1,0:T(4,128)S(1)} %bitcast.16, s32[4,64]{1,0:T(4,128)S(1)} %bitcast.18, s32[4,64]{1,0:T(4,128)S(1)} %bitcast.20, bf16[24,4608]{1,0:T(8,128)(2,1)S(1)} %bitcast.12), custom_call_target="tpu_custom_call" | custom-call | tf_op jit(solution)/shard_map/bands/pallas_call | solution.py:561
  29.0 0.0 copy-start.1
  29.0 0.0 copy-start.2
  29.1 0.0 copy-start.8
  29.1 0.0 copy-start.9
  29.1 0.0 copy-start.10
  29.1 0.0 copy-start.11
  29.1 0.0 copy-start.12
  29.1 1.2 %copy.18.wp_ref = bf16[768,192]{1,0:T(8,128)(2,1)S(1)} copy(bf16[768,192]{0,1:T(8,128)(2,1)} %param.27) | data formatting | bytes 589824 | tf_op args[12]
  30.3 0.0 copy-done.3
  30.3 0.0 copy-done.1
  30.4 0.0 copy-done.2
  30.4 0.0 copy-done.8
  30.4 0.0 copy-done.9
  30.4 0.0 copy-done.10
  30.4 0.0 copy-done.11
  30.4 0.0 copy-done.12
  30.4 15.0 %block.1 = (bf16[24,4608]{1,0:T(8,128)(2,1)}, f32[576,192]{1,0:T(8,128)S(1)}, bf16[288,192]{1,0:T(8,128)(2,1)S(1)}, bf16[2,2,48,768]{3,2,1,0:T(8,128)(2,1)S(1)}, bf16[2,2,96,384]{3,2,1,0:T(8,128)(2,1)S(1)}) custom-call(s32[64]{0:T(128)S(1)} %copy-done.7, bf16[24,4608]{1,0:T(8,128)(2,1)S(1)} %bitcast.13, bf16[24,4608]{1,0:T(8,128)(2,1)S(1)} %bitcast.14, ...), custom_call_target="tpu_custom_call" | custom-call | tf_op jit(solution)/shard_map/block/pallas_call | solution.py:572
  45.4 44.4 %finish.1 = (bf16[24,4608]{1,0:T(8,128)(2,1)S(1)}, f32[1,288]{1,0:T(1,128)S(1)}) custom-call(s32[64]{0:T(128)S(1)} %copy-done.7, s32[4,64]{1,0:T(4,128)S(1)} %bitcast.17, s32[4,64]{1,0:T(4,128)S(1)} %bitcast.19, s32[4,64]{1,0:T(4,128)S(1)} %bitcast.21, bf16[2,2,48,768]{3,2,1,0:T(8,128)(2,1)S(1)} %get-tuple-element.11.gi_ref, ...), custom_call_target="tpu_custom_call" | custom-call | tf_op jit(solution)/shard_map/finish/pallas_call | solution.py:616
  89.8 0.6 reduce
  90.4 0.7 copy.20
  (4 shorter events, 0.0 us)
Async XLA Ops:
  0.6 0.7 copy-start.13
  1.3 0.9 copy-start.4
  1.3 0.9 copy-start.5
  1.3 0.9 copy-start.6
  1.3 0.9 copy-start.7
  2.2 0.9 %copy-start = (bf16[1,1,24,4608]{3,2,1,0:T(8,128)(2,1)S(1)}, bf16[1,1,24,4608]{3,2,1,0:T(8,128)(2,1)}, u32[]{:S(2)}) copy-start(bf16[1,1,24,4608]{3,2,1,0:T(8,128)(2,1)} %param.15) | copy-start | bytes 663556
  3.2 27.1 %copy-start.3 = (bf16[1,1,24,4608]{3,2,1,0:T(8,128)(2,1)S(1)}, bf16[1,1,24,4608]{3,2,1,0:T(8,128)(2,1)}, u32[]{:S(2)}) copy-start(bf16[1,1,24,4608]{3,2,1,0:T(8,128)(2,1)} %param.16) | copy-start | bytes 663556
  29.0 1.3 %copy-start.1 = (bf16[1,1,24,4608]{3,2,1,0:T(8,128)(2,1)S(1)}, bf16[1,1,24,4608]{3,2,1,0:T(8,128)(2,1)}, u32[]{:S(2)}) copy-start(bf16[1,1,24,4608]{3,2,1,0:T(8,128)(2,1)} %param.15) | copy-start | bytes 663556
  29.0 1.3 %copy-start.2 = (bf16[192,768]{1,0:T(8,128)(2,1)S(1)}, bf16[192,768]{1,0:T(8,128)(2,1)}, u32[]{:S(2)}) copy-start(bf16[192,768]{1,0:T(8,128)(2,1)} %we_ref.1) | copy-start | bytes 884740
  29.1 1.3 %copy-start.8 = (f32[192]{0:T(256)S(1)}, f32[192]{0:T(256)}, u32[]{:S(2)}) copy-start(f32[192]{0:T(256)} %param.22) | copy-start | bytes 2308
  29.1 1.3 %copy-start.9 = (f32[192]{0:T(256)S(1)}, f32[192]{0:T(256)}, u32[]{:S(2)}) copy-start(f32[192]{0:T(256)} %param.23) | copy-start | bytes 2308
  29.1 1.3 %copy-start.10 = (f32[192]{0:T(256)S(1)}, f32[192]{0:T(256)}, u32[]{:S(2)}) copy-start(f32[192]{0:T(256)} %param.24) | copy-start | bytes 2308
  29.1 1.3 %copy-start.11 = (f32[192]{0:T(256)S(1)}, f32[192]{0:T(256)}, u32[]{:S(2)}) copy-start(f32[192]{0:T(256)} %param.28) | copy-start | bytes 2308
  29.1 1.3 %copy-start.12 = (f32[192]{0:T(256)S(1)}, f32[192]{0:T(256)}, u32[]{:S(2)}) copy-start(f32[192]{0:T(256)} %param.29) | copy-start | bytes 2308

commit v2 on v1

--- a/solution.py
+++ b/solution.py
@@ -117,25 +117,26 @@
         ).astype(BF16)
 
 
-def block_kernel(
+def main_kernel(
     rows_ref,
+    step_ref,
+    code_ref,
+    shift_ref,
     x_ref,
     c_ref,
     halo_ref,
     kern_ref,
     bias_ref,
     gain_ref,
-    shift_ref,
+    nbias_ref,
     we_ref,
     be_ref,
     wp_ref,
     bp_ref,
     ls_ref,
     out_ref,
-    base_ref,
-    dh_ref,
-    gi_ref,
-    gp_ref,
+    ig_ref,
+    wg_ref,
     weights,
     ext,
     ext_at,
@@ -149,11 +150,78 @@
     d_pad,
     d_at,
     d_ext,
+    base_ref,
+    dh_ref,
+    gi_ref,
+    gp_ref,
+    dh_lo,
+    dh_hi,
+    core_i,
+    core_p,
+    xs_i,
+    xs_p,
+    xr_i,
+    xr_p,
+    own_x_i,
+    own_x_p,
+    y_send_buf,
+    y_recv_buf,
+    z_send_buf,
+    z_recv_buf,
+    dh_send,
+    dh_recv,
+    core_send,
+    core_recv,
+    x_send,
+    x_recv,
+    y_send,
+    y_recv,
+    z_send,
+    z_recv,
 ):
-    tile_len = rows_ref[lax.axis_index("space")]
+    me = lax.axis_index("space")
+    dp = lax.axis_index("dp")
+    mx = dp // 4
+    core = lax.rem(dp, 2)
+    my = (me // 32) * 2 + lax.rem(dp // 2, 2)
+    z = lax.rem(me, 32)
+    hi = lax.rem(me + 1, TILES)
+    lo = lax.rem(me + TILES - 1, TILES)
+    other = dp + 1 - 2 * core
+
+    def at_x(x):
+        return (x * 4 + lax.rem(dp, 4), me)
+
+    def at_y(y):
+        return (mx * 4 + lax.rem(y, 2) * 2 + core, (y // 2) * 32 + z)
+
+    def at_z(other_z):
+        return (dp, me - z + other_z)
+
+    xs = [lax.rem(mx + d, 4) for d in (1, 2, 3)]
+    ys = [lax.rem(my + d, 4) for d in (1, 2, 3)]
+    far_first = sorted(range(1, 32), key=lambda d: -min(d, 32 - d))
+    zs = [lax.rem(z + d, 32) for d in far_first]
+    peers = [at_z(other_z) for other_z in zs] + [at_y(y) for y in ys] + [at_x(x) for x in xs]
+    peers += [(dp, lo), (dp, hi), (other, me)]
+    barrier = pltpu.get_barrier_semaphore()
+    for peer in peers:
+        pl.semaphore_signal(barrier, inc=1, device_id=peer, device_id_type=MESH)
+
+    def remote(source, landing, send, recv, peer):
+        return pltpu.make_async_remote_copy(
+            src_ref=source,
+            dst_ref=landing,
+            send_sem=send,
+            recv_sem=recv,
+            device_id=peer,
+            device_id_type=MESH,
+        )
+
+    tile_len = rows_ref[me]
     inside = iota((TS, C), 0) < tile_len
     for t in range(49):
-        weights[t] = jnp.broadcast_to(kern_ref[t : t + 1, :], (8, C))
+        weights[t] = jnp.broadcast_to(kern_ref[t // 7, t % 7 : t % 7 + 1, :], (8, C))
 
     halo = halo_ref[...].astype(F32)
     col = iota((1, 144), 1)
@@ -201,7 +269,7 @@
         scaled = centred * inverse
         normal[rows, :] = scaled
         rstd[rows, :] = jnp.broadcast_to(inverse, (96, 128))
-        normed[rows, :] = (scaled * gain_ref[...] + shift_ref[...]).astype(BF16)
+        normed[rows, :] = (scaled * gain_ref[...] + nbias_ref[...]).astype(BF16)
 
     grads = [jnp.where(inside, column, 0.0) for column in columns_of(c_ref)]
     for j in range(TS):
@@ -211,13 +279,13 @@
     grad_in, grad_proj = [], []
     for chunk in range(3):
         hidden = slice(256 * chunk, 256 * chunk + 256)
-        pre = dot(normed[...], we_ref[:, hidden]) + be_ref[:, hidden]
+        pre = dot(normed[...], we_ref[:, hidden]) + be_ref[hidden][None, :]
         phi = 0.5 * (1.0 + lax.erf(pre * ROOT_HALF))
         act = (pre * phi).astype(BF16)
         slope = phi + pre * INV_ROOT_TAU * jnp.exp(-0.5 * pre * pre)
-        d_act = dot_tb(d_branch[...], wp_ref[hidden, :])
+        d_act = dot(d_branch[...], wp_ref[:, hidden])
         d_pre = (d_act * slope).astype(BF16)
-        forward = dot(act, wp_ref[hidden, :])
+        forward = dot_tb(act, wp_ref[:, hidden])
         backward = dot_tb(d_pre, we_ref[:, hidden])
         if chunk == 0:
             branch[...] = forward
@@ -229,14 +297,23 @@
         grad_proj.append(dot_ta(act, d_branch[...]) * SCALE)
     grad_in = jnp.concatenate(grad_in, axis=1)
     grad_proj = jnp.concatenate(grad_proj, axis=0)
-    for core in range(2):
+    for half in range(2):
         for x in range(2):
-            gi_ref[core, x] = jnp.concatenate(
-                [grad_in[24 * d : 24 * d + 24] for d in (4 * x + core, 4 * x + 2 + core)], axis=0
+            gi_ref[half, x] = jnp.concatenate(
+                [grad_in[24 * d : 24 * d + 24] for d in (4 * x + half, 4 * x + 2 + half)], axis=0
             ).astype(BF16)
-            gp_ref[core, x] = jnp.concatenate(
-                [grad_proj[96 * d : 96 * d + 96] for d in (4 * x + core, 4 * x + 2 + core)], axis=1
+            gp_ref[half, x] = jnp.concatenate(
+                [grad_proj[96 * d : 96 * d + 96] for d in (4 * x + half, 4 * x + 2 + half)], axis=1
             ).astype(BF16)
+
+
+    pl.semaphore_wait(barrier, len(peers))
+    core_copies = [
+        remote(gi_ref.at[1 - core], core_i, core_send.at[0], core_recv.at[0], (other, me)),
+        remote(gp_ref.at[1 - core], core_p, core_send.at[1], core_recv.at[1], (other, me)),
+    ]
+    for copy in core_copies:
+        copy.start()
 
     for p, (left, right) in enumerate(zip(*[iter(columns_of(x_ref))] * 2)):
         pair = []
@@ -257,6 +334,31 @@
         value = rstd[rows, 0:1] * (grad - mean - scaled * along)
         for j in range(4):
             d_pad[block * 4 + j + 6, 8:32] = value[j * TS : j * TS + TS]
+
+    for copy in core_copies:
+        copy.wait()
+    for x in range(2):
+        sum_i = gi_ref[core, x].astype(F32) + core_i[x].astype(F32)
+        sum_p = gp_ref[core, x].astype(F32) + core_p[x].astype(F32)
+        own_x_i[x] = sum_i
+        own_x_p[x] = sum_p
+        xs_i[x] = sum_i.astype(BF16)
+        xs_p[x] = sum_p.astype(BF16)
+
+    def x_copy(n, x, wide):
+        if wide:
+            return remote(xs_i.at[x], xr_i.at[n], x_send.at[n], x_recv.at[n], at_x(x))
+        return remote(xs_p.at[x - 2], xr_p.at[n], x_send.at[n], x_recv.at[n], at_x(x))
+
+    for n, x in enumerate(xs):
+
+        @pl.when(x < 2)
+        def _():
+            x_copy(n, x, True).start()
+
+        @pl.when(x >= 2)
+        def _():
+            x_copy(n, x, False).start()
 
     @pl.loop(0, 36)
     def _(at):
@@ -292,142 +394,67 @@
             d_ext[27 + k, 3:27],
         ]
     dh_ref[...] = jnp.concatenate(parts, axis=0).astype(BF16)
-    for j in range(TS):
-        base_ref[j * TS : j * TS + TS, :] += d_ext[3 + j, 3:27]
-
-
-def finish_kernel(
-    rows_ref,
-    step_ref,
-    code_ref,
-    shift_ref,
-    gi_ref,
-    gp_ref,
-    dh_ref,
-    base_ref,
-    ig_ref,
-    wg_ref,
-    dh_lo,
-    dh_hi,
-    core_i,
-    core_p,
-    xs_i,
-    xs_p,
-    xr_i,
-    xr_p,
-    ys_i,
-    ys_p,
-    yr_i,
-    yr_p,
-    hs_i,
-    hs_p,
-    hr_i,
-    hr_p,
-    ls_i,
-    ls_p,
-    lr_i,
-    lr_p,
-    own_x_i,
-    own_x_p,
-    own_y_i,
-    own_y_p,
-    own_h_i,
-    own_h_p,
-    dh_send,
-    dh_recv,
-    core_send,
-    core_recv,
-    x_send,
-    x_recv,
-    y_send,
-    y_recv,
-    h_send,
-    h_recv,
-    l_send,
-    l_recv,
-):
-    me = lax.axis_index("space")
-    dp = lax.axis_index("dp")
-    mx = dp // 4
-    core = lax.rem(dp, 2)
-    my = (me // 32) * 2 + lax.rem(dp // 2, 2)
-    z = lax.rem(me, 32)
-    mh = z // 8
-    ml = lax.rem(z, 8)
-    hi = lax.rem(me + 1, TILES)
-    lo = lax.rem(me + TILES - 1, TILES)
-    other = dp + 1 - 2 * core
-
-    def at_x(x):
-        return (x * 4 + lax.rem(dp, 4), me)
-
-    def at_y(y):
-        return (mx * 4 + lax.rem(y, 2) * 2 + core, (y // 2) * 32 + z)
-
-    def at_h(h):
-        return (dp, (me // 32) * 32 + h * 8 + ml)
-
-    def at_l(lane):
-        return (dp, (me // 8) * 8 + lane)
-
-    xs = [lax.rem(mx + d, 4) for d in (1, 2, 3)]
-    ys = [lax.rem(my + d, 4) for d in (1, 2, 3)]
-    hs = [lax.rem(mh + d, 4) for d in (1, 2, 3)]
-    lanes = [lax.rem(ml + d, 8) for d in range(1, 8)]
-    peers = [(dp, lo), (dp, hi), (other, me)]
-    peers += [at_x(x) for x in xs] + [at_y(y) for y in ys]
-    peers += [at_h(h) for h in hs] + [at_l(lane) for lane in lanes]
-    barrier = pltpu.get_barrier_semaphore()
-    for peer in peers:
-        pl.semaphore_signal(barrier, inc=1, device_id=peer, device_id_type=MESH)
-    pl.semaphore_wait(barrier, len(peers))
-
-    def remote(source, landing, send, recv, peer):
-        return pltpu.make_async_remote_copy(
-            src_ref=source,
-            dst_ref=landing,
-            send_sem=send,
-            recv_sem=recv,
-            device_id=peer,
-            device_id_type=MESH,
-        )
-
-    core_copies = [
-        remote(gi_ref.at[1 - core], core_i, core_send.at[0], core_recv.at[0], (other, me)),
-        remote(gp_ref.at[1 - core], core_p, core_send.at[1], core_recv.at[1], (other, me)),
-    ]
     dh_copies = [
         remote(dh_ref, dh_lo, dh_send.at[0], dh_recv.at[0], (dp, hi)),
         remote(dh_ref, dh_hi, dh_send.at[1], dh_recv.at[1], (dp, lo)),
     ]
-    for copy in core_copies + dh_copies:
+    for copy in dh_copies:
         copy.start()
-    for copy in core_copies:
-        copy.wait()
-    for x in range(2):
-        sum_i = gi_ref[core, x].astype(F32) + core_i[x].astype(F32)
-        sum_p = gp_ref[core, x].astype(F32) + core_p[x].astype(F32)
-        own_x_i[x] = sum_i
-        own_x_p[x] = sum_p
-        xs_i[x] = sum_i.astype(BF16)
-        xs_p[x] = sum_p.astype(BF16)
-
-    def x_copy(n, x, wide):
+
+    def regroup(wide):
         if wide:
-            return remote(xs_i.at[x], xr_i.at[n], x_send.at[n], x_recv.at[n], at_x(x))
-        return remote(xs_p.at[x - 2], xr_p.at[n], x_send.at[n], x_recv.at[n], at_x(x))
-
-    for n, x in enumerate(xs):
-
-        @pl.when(x < 2)
-        def _():
-            x_copy(n, x, True).start()
-
-        @pl.when(x >= 2)
-        def _():
-            x_copy(n, x, False).start()
-
-    tile_len = rows_ref[me]
+            total = own_x_i[mx]
+            for n in range(3):
+                total = total + xr_i[n].astype(F32)
+        else:
+            total = own_x_p[mx - 2]
+            for n in range(3):
+                total = total + xr_p[n].astype(F32)
+        total = total.astype(BF16)
+        run = iota((24, 1), 0)
+        height = 48 if wide else 96
+        runs = None
+        for part in range(8 if wide else 4):
+            rows = []
+            for y in range(4):
+                for h in range(4):
+                    if wide:
+                        row = jnp.where(run % 8 == part, 24 * (y % 2) + 12 * (y // 2) + 3 * h + run // 8, -1)
+                    elif part // 2 == y % 2:
+                        row = jnp.where(run % 2 == part % 2, 48 * (y // 2) + 12 * h + run // 2, -1)
+                    else:
+                        row = jnp.full((24, 1), -1, jnp.int32)
+                    rows.append(row)
+            pick = one_hot(iota((384, height), 1), jnp.concatenate(rows, axis=0))
+            term = dot(pick, total[:, 96 * part : 96 * part + 96])
+            runs = term if runs is None else runs + term
+        for y in range(4):
+            at_y = [runs[96 * y + 24 * h : 96 * y + 24 * h + 24] for h in range(4)]
+            y_send_buf[y] = jnp.concatenate(at_y, axis=1).astype(BF16)
+
+    @pl.when(mx < 2)
+    def _():
+        for n, x in enumerate(xs):
+            remote(xs_i.at[0], xr_i.at[n], x_send.at[n], x_recv.at[n], at_x(x)).wait_recv()
+        regroup(True)
+
+    @pl.when(mx >= 2)
+    def _():
+        for n, x in enumerate(xs):
+            remote(xs_p.at[0], xr_p.at[n], x_send.at[n], x_recv.at[n], at_x(x)).wait_recv()
+        regroup(False)
+
+    y_copies = [
+        remote(y_send_buf.at[y], y_recv_buf.at[n], y_send.at[n], y_recv.at[n], at_y(y))
+        for n, y in enumerate(ys)
+    ]
+    for copy in y_copies:
+        copy.start()
+
+    for j in range(TS):
+        base_ref[j * TS : j * TS + TS, :] += d_ext[3 + j, 3:27]
+
+
     spread = []
     lane = iota((1, 96), 1)
     for source in range(3):
@@ -442,6 +469,21 @@
         spread.append(one_hot(iota((96, 96), 0), target))
     cell = jnp.concatenate(band_cells(tile_len), axis=0)
     to_bands = one_hot(iota((288, CELLS), 1), cell)
+    for copy in y_copies:
+        copy.wait()
+    total = y_send_buf[my].astype(F32)
+    for n in range(3):
+        total = total + y_recv_buf[n].astype(F32)
+    for h in range(4):
+        for row in range(8):
+            z_send_buf[8 * h + row] = total[3 * row : 3 * row + 3, 96 * h : 96 * h + 96].astype(BF16)
+    z_copies = [
+        remote(z_send_buf.at[other_z], z_recv_buf.at[n], z_send, z_recv, at_z(other_z))
+        for n, other_z in enumerate(zs)
+    ]
+    for copy in z_copies:
+        copy.start()
+
     for copy in dh_copies:
         copy.wait()
     parts = []
@@ -463,68 +505,11 @@
             inside, jnp.concatenate(pair, axis=1), 0.0
         ).astype(BF16)
 
-    def exchange(peers_at, send_refs, recv_ref, send, recv):
-        copies = []
-        for n, (source, device) in enumerate(zip(send_refs, peers_at)):
-            copies.append(remote(source, recv_ref.at[n], send.at[n], recv.at[n], device))
-        for copy in copies:
-            copy.start()
-        for copy in copies:
-            copy.wait()
-
-    def tail(wide, own_x, xr, own_y, ysend, yr, own_h, hsend, hr, lsend, lr):
-        total = own_x[mx if wide else mx - 2]
-        for n in range(3):
-            total = total + xr[n].astype(F32)
-        count = 12 if wide else 48
-        for y in range(4):
-            if wide:
-                part = total[24 * (y % 2) + 12 * (y // 2) :][:12]
-            else:
-                part = total[48 * (y // 2) :][:48, C * (y % 2) :][:, :C]
-            own_y[y, 0:count] = part
-            ysend[y, 0:count] = part.astype(BF16)
-        exchange([at_y(y) for y in ys], [ysend.at[y] for y in ys], yr, y_send, y_recv)
-        total = own_y[my, 0:count]
-        for n in range(3):
-            total = total + yr[n, 0:count].astype(F32)
-        count = count // 4
-        for h in range(4):
-            part = total[h * count : h * count + count]
-            own_h[h, 0:count] = part
-            hsend[h, 0:count] = part.astype(BF16)
-        exchange([at_h(h) for h in hs], [hsend.at[h] for h in hs], hr, h_send, h_recv)
-        total = own_h[mh, 0:count]
-        for n in range(3):
-            total = total + hr[n, 0:count].astype(F32)
-        lsend[0:count] = total.astype(BF16)
-        exchange([at_l(lane) for lane in lanes], [lsend] * 7, lr, l_send, l_recv)
-        for n in range(7):
-            total = total + lr[n, 0:count].astype(F32)
-        width = total.shape[1]
-        for m in range(8):
-            pieces, at = [], 288 * m
-            while at < 288 * m + 288:
-                row, first = at // width, at % width
-                size = min(288 * m + 288 - at, width - first)
-                pieces.append(total[row : row + 1, first : first + size])
-                at += size
-
-            @pl.when(ml == m)
-            def _():
-                wg_ref[...] = jnp.concatenate(pieces, axis=1) if len(pieces) > 1 else pieces[0]
-
-    @pl.when(mx < 2)
-    def _():
-        for n, x in enumerate(xs):
-            remote(xs_i.at[0], xr_i.at[n], x_send.at[n], x_recv.at[n], at_x(x)).wait_recv()
-        tail(True, own_x_i, xr_i, own_y_i, ys_i, yr_i, own_h_i, hs_i, hr_i, ls_i, lr_i)
-
-    @pl.when(mx >= 2)
-    def _():
-        for n, x in enumerate(xs):
-            remote(xs_p.at[0], xr_p.at[n], x_send.at[n], x_recv.at[n], at_x(x)).wait_recv()
-        tail(False, own_x_p, xr_p, own_y_p, ys_p, yr_p, own_h_p, hs_p, hr_p, ls_p, lr_p)
+    remote(z_recv_buf, z_recv_buf, z_send, z_recv, (other, me)).wait()
+    total = z_send_buf[z].astype(F32)
+    for n in range(31):
+        total = total + z_recv_buf[n].astype(F32)
+    wg_ref[...] = jnp.concatenate([total[t : t + 1] for t in range(3)], axis=1)
 
     for n, x in enumerate(xs):
 
@@ -569,59 +554,34 @@
         ),
         name="bands",
     )(tile_rows, *tables, x)
-    out, base, dh, gi, gp = pl.pallas_call(
-        block_kernel,
+    vm = pltpu.VMEM
+    out, ig, wg = pl.pallas_call(
+        main_kernel,
         out_shape=(
             jax.ShapeDtypeStruct((TS, WIDE), BF16),
-            jax.ShapeDtypeStruct((CELLS, C), F32),
-            jax.ShapeDtypeStruct((288, C), BF16),
-            jax.ShapeDtypeStruct((2, 2, 48, H), BF16),
-            jax.ShapeDtypeStruct((2, 2, 96, PAIR), BF16),
-        ),
-        in_specs=[SMEM] + [VMEM] * 12,
-        out_specs=(VMEM,) * 5,
-        scratch_shapes=[
-            pltpu.VMEM((49, 8, C), F32),
-            pltpu.VMEM((30, 40, C), F32),
-            pltpu.VMEM((7, 30, TS, C), F32),
-            pltpu.VMEM((CELLS, C), F32),
-            pltpu.VMEM((CELLS, C), F32),
-            pltpu.VMEM((CELLS, 128), F32),
-            pltpu.VMEM((CELLS, C), BF16),
-            pltpu.VMEM((CELLS, C), BF16),
-            pltpu.VMEM((CELLS, C), F32),
-            pltpu.VMEM((CELLS, C), F32),
-            pltpu.VMEM((36, 40, C), F32),
-            pltpu.VMEM((7, 36, 32, C), F32),
-            pltpu.VMEM((30, 32, C), F32),
-        ],
-        compiler_params=pltpu.CompilerParams(vmem_limit_bytes=48 << 20),
-        name="block",
-    )(
-        tile_rows,
-        x,
-        c,
-        halo,
-        conv_kernel.reshape(49, C),
-        conv_bias.reshape(1, C),
-        norm_gain.reshape(1, C),
-        norm_bias.reshape(1, C),
-        w_expand,
-        b_expand.reshape(1, H),
-        w_project,
-        b_project.reshape(1, C),
-        layer_scale.reshape(1, C),
-    )
-    vm = pltpu.VMEM
-    ig, wg = pl.pallas_call(
-        finish_kernel,
-        out_shape=(
             jax.ShapeDtypeStruct((TS, WIDE), BF16),
             jax.ShapeDtypeStruct((1, 288), F32),
         ),
-        in_specs=[SMEM] * 4 + [VMEM] * 4,
-        out_specs=(VMEM, VMEM),
+        in_specs=[SMEM] * 4 + [VMEM] * 12,
+        out_specs=(VMEM,) * 3,
         scratch_shapes=[
+            vm((49, 8, C), F32),
+            vm((30, 40, C), F32),
+            vm((7, 30, TS, C), F32),
+            vm((CELLS, C), F32),
+            vm((CELLS, C), F32),
+            vm((CELLS, 128), F32),
+            vm((CELLS, C), BF16),
+            vm((CELLS, C), BF16),
+            vm((CELLS, C), F32),
+            vm((CELLS, C), F32),
+            vm((36, 40, C), F32),
+            vm((7, 36, 32, C), F32),
+            vm((30, 32, C), F32),
+            vm((CELLS, C), F32),
+            vm((288, C), BF16),
+            vm((2, 2, 48, H), BF16),
+            vm((2, 2, 96, PAIR), BF16),
             vm((288, C), BF16),
             vm((288, C), BF16),
             vm((2, 48, H), BF16),
@@ -630,33 +590,36 @@
             vm((2, 96, PAIR), BF16),
             vm((3, 48, H), BF16),
             vm((3, 96, PAIR), BF16),
-            vm((4, 16, H), BF16),
-            vm((4, 48, C), BF16),
-            vm((3, 16, H), BF16),
-            vm((3, 48, C), BF16),
-            vm((4, 16, H), BF16),
-            vm((4, 16, C), BF16),
-            vm((3, 16, H), BF16),
-            vm((3, 16, C), BF16),
-            vm((16, H), BF16),
-            vm((16, C), BF16),
-            vm((7, 16, H), BF16),
-            vm((7, 16, C), BF16),
             vm((2, 48, H), F32),
             vm((2, 96, PAIR), F32),
-            vm((4, 16, H), F32),
-            vm((4, 48, C), F32),
-            vm((4, 16, H), F32),
-            vm((4, 16, C), F32),
+            vm((4, 24, PAIR), BF16),
+            vm((3, 24, PAIR), BF16),
+            vm((32, 3, 96), BF16),
+            vm((31, 3, 96), BF16),
         ]
         + [dma((2,))] * 4
-        + [dma((3,))] * 6
-        + [dma((7,))] * 2,
+        + [dma((3,))] * 4
+        + [dma] * 2,
         compiler_params=pltpu.CompilerParams(
-            collective_id=1, has_side_effects=True, vmem_limit_bytes=32 << 20
+            collective_id=1, has_side_effects=True, vmem_limit_bytes=52 << 20
         ),
-        name="finish",
-    )(tile_rows, *tables, gi, gp, dh, base)
+        name="main",
+    )(
+        tile_rows,
+        *tables,
+        x,
+        c,
+        halo,
+        conv_kernel,
+        conv_bias.reshape(1, C),
+        norm_gain.reshape(1, C),
+        norm_bias.reshape(1, C),
+        w_expand,
+        b_expand,
+        w_project.T,
+        b_project.reshape(1, C),
+        layer_scale.reshape(1, C),
+    )
     return (
         out.reshape(1, 1, TS, WIDE),
         ig.reshape(1, 1, TS, WIDE),

time: 91.4 us -> 70.9 us (0.78)
  the two profiles are of different devices: /device:TPU:1 before, /device:TPU:2 now
where the time goes in v2:
time: 70.9 us; the launch traced here: 70.6 us
  Pallas kernels  63.3 us (89%)
  local copies, waits for them, and re-layouts  5.87 us (8%)
  between operations  0.8 us (1%)
    pallas_call x1, Pallas kernels, local(): pl.pallas_call(main_kernel, out_shape=(jax.ShapeDtypeStruct((TS, WIDE), B...  37.4 us
    pallas_call x1, Pallas kernels, local(): pl.pallas_call(bands_kernel, out_shape=jax.ShapeDtypeStruct((288, C), BF1...  25.9 us
    unnamed x34, local copies, waits for them, and re-layouts  5.87 us

profile of v2, /device:TPU:2, one launch (start us, length us, event | category | flops | bytes accessed | tf_op | source)
XLA Modules:
  0.0 70.6 jit_solution(1930125981960020600)
XLA Ops:
  0.6 0.0 copy-start.8
  0.6 0.0 copy-start.7
  0.7 0.0 copy-start.6
  0.7 0.0 copy-start.10
  0.7 0.6 copy-done.8
  1.3 0.0 copy-done.7
  1.3 0.0 copy-done.6
  1.3 0.0 copy-done.10
  1.4 0.0 copy-start
  1.4 0.9 %copy-done = bf16[1,1,24,4608]{3,2,1,0:T(8,128)(2,1)S(1)} copy-done((bf16[1,1,24,4608]{3,2,1,0:T(8,128)(2,1)S(1)}, bf16[1,1,24,4608]{3,2,1,0:T(8,128)(2,1)}, u32[]{:S(2)}) %copy-start) | copy-done | bytes 221208
  2.3 0.0 copy-start.1
  2.3 0.0 copy-start.12
  2.3 0.0 copy-start.13
  2.3 0.0 copy-start.14
  2.3 0.0 copy-start.15
  2.3 25.9 %bands.1.halo_ref = bf16[288,192]{1,0:T(8,128)(2,1)S(1)} custom-call(s32[64]{0:T(128)S(1)} %copy-done.10, s32[4,64]{1,0:T(4,128)S(1)} %bitcast.19, s32[4,64]{1,0:T(4,128)S(1)} %bitcast.21, s32[4,64]{1,0:T(4,128)S(1)} %bitcast.23, bf16[24,4608]{1,0:T(8,128)(2,1)S(1)} %bitcast.13), custom_call_target="tpu_custom_call" | custom-call | tf_op jit(solution)/shard_map/bands/pallas_call | solution.py:546
  28.2 0.0 copy-done.1
  28.2 0.0 copy-done.5
  28.2 0.0 copy-done.9
  28.3 0.0 copy-done.11
  28.3 0.0 copy-done.12
  28.3 0.0 copy-done.13
  28.3 0.0 copy-done.14
  28.3 0.0 copy-done.15
  28.3 0.0 copy-start.2
  28.3 1.0 %copy-done.2 = bf16[192,768]{1,0:T(8,128)(2,1)S(1)} copy-done((bf16[192,768]{1,0:T(8,128)(2,1)S(1)}, bf16[192,768]{1,0:T(8,128)(2,1)}, u32[]{:S(2)}) %copy-start.2) | copy-done | bytes 294936
  29.3 1.0 %copy-done.3 = bf16[768,192]{0,1:T(8,128)(2,1)S(1)} copy-done((bf16[768,192]{0,1:T(8,128)(2,1)S(1)}, bf16[768,192]{0,1:T(8,128)(2,1)}, u32[]{:S(2)}) %copy-start.3) | copy-done | bytes 294936
  30.2 0.9 %copy-done.4 = bf16[1,1,24,4608]{3,2,1,0:T(8,128)(2,1)S(1)} copy-done((bf16[1,1,24,4608]{3,2,1,0:T(8,128)(2,1)S(1)}, bf16[1,1,24,4608]{3,2,1,0:T(8,128)(2,1)}, u32[]{:S(2)}) %copy-start.4) | copy-done | bytes 221208
  31.2 37.4 %main.1 = (bf16[24,4608]{1,0:T(8,128)(2,1)S(1)}, bf16[24,4608]{1,0:T(8,128)(2,1)S(1)}, f32[1,288]{1,0:T(1,128)S(1)}) custom-call(s32[64]{0:T(128)S(1)} %copy-done.10, s32[4,64]{1,0:T(4,128)S(1)} %bitcast.20, s32[4,64]{1,0:T(4,128)S(1)} %bitcast.22, s32[4,64]{1,0:T(4,128)S(1)} %bitcast.24, bf16[24,4608]{1,0:T(8,128)(2,1)S(1)} %bitcast.14, ...), custom_call_target="tpu_custom_call" | custom-call | tf_op jit(solution)/shard_map/main/pallas_call | solution.py:558
  68.6 0.6 reduce
  69.2 0.7 copy.20
  69.9 0.7 copy.21
  (5 shorter events, 0.0 us)
Async XLA Ops:
  0.6 0.7 copy-start.8
  0.6 0.7 copy-start.7
  0.7 0.7 copy-start.6
  0.7 0.7 copy-start.10
  1.4 0.9 %copy-start = (bf16[1,1,24,4608]{3,2,1,0:T(8,128)(2,1)S(1)}, bf16[1,1,24,4608]{3,2,1,0:T(8,128)(2,1)}, u32[]{:S(2)}) copy-start(bf16[1,1,24,4608]{3,2,1,0:T(8,128)(2,1)} %param.15) | copy-start | bytes 663556
  2.3 25.9 %copy-start.1 = (bf16[1,1,24,4608]{3,2,1,0:T(8,128)(2,1)S(1)}, bf16[1,1,24,4608]{3,2,1,0:T(8,128)(2,1)}, u32[]{:S(2)}) copy-start(bf16[1,1,24,4608]{3,2,1,0:T(8,128)(2,1)} %param.15) | copy-start | bytes 663556
  2.3 25.9 %copy-start.5 = (f32[7,7,192]{2,1,0:T(8,128)S(1)}, f32[7,7,192]{2,1,0:T(8,128)}, u32[]{:S(2)}) copy-start(f32[7,7,192]{2,1,0:T(8,128)} %kern_ref.1) | copy-start | bytes 112900
  2.3 26.0 %copy-start.9 = (f32[768]{0:T(1024)S(1)}, f32[768]{0:T(1024)}, u32[]{:S(2)}) copy-start(f32[768]{0:T(1024)} %be_ref.1) | copy-start | bytes 9220
  2.3 26.0 %copy-start.11 = (f32[192]{0:T(256)S(1)}, f32[192]{0:T(256)}, u32[]{:S(2)}) copy-start(f32[192]{0:T(256)} %param.22) | copy-start | bytes 2308
  2.3 26.0 %copy-start.12 = (f32[192]{0:T(256)S(1)}, f32[192]{0:T(256)}, u32[]{:S(2)}) copy-start(f32[192]{0:T(256)} %param.23) | copy-start | bytes 2308
  2.3 26.0 %copy-start.13 = (f32[192]{0:T(256)S(1)}, f32[192]{0:T(256)}, u32[]{:S(2)}) copy-start(f32[192]{0:T(256)} %param.24) | copy-start | bytes 2308
  2.3 26.0 %copy-start.14 = (f32[192]{0:T(256)S(1)}, f32[192]{0:T(256)}, u32[]{:S(2)}) copy-start(f32[192]{0:T(256)} %param.28) | copy-start | bytes 2308
  2.3 26.0 %copy-start.15 = (f32[192]{0:T(256)S(1)}, f32[192]{0:T(256)}, u32[]{:S(2)}) copy-start(f32[192]{0:T(256)} %param.29) | copy-start | bytes 2308
  28.3 1.0 %copy-start.2 = (bf16[192,768]{1,0:T(8,128)(2,1)S(1)}, bf16[192,768]{1,0:T(8,128)(2,1)}, u32[]{:S(2)}) copy-start(bf16[192,768]{1,0:T(8,128)(2,1)} %we_ref.1) | copy-start | bytes 884740
  29.3 1.0 %copy-start.3 = (bf16[768,192]{0,1:T(8,128)(2,1)S(1)}, bf16[768,192]{0,1:T(8,128)(2,1)}, u32[]{:S(2)}) copy-start(bf16[768,192]{0,1:T(8,128)(2,1)} %param.27) | copy-start | bytes 884740
  30.2 0.9 %copy-start.4 = (bf16[1,1,24,4608]{3,2,1,0:T(8,128)(2,1)S(1)}, bf16[1,1,24,4608]{3,2,1,0:T(8,128)(2,1)}, u32[]{:S(2)}) copy-start(bf16[1,1,24,4608]{3,2,1,0:T(8,128)(2,1)} %param.16) | copy-start | bytes 663556

commit v3 on v2

--- a/solution.py
+++ b/solution.py
@@ -23,6 +23,8 @@
 MESH = pl.DeviceIdType.MESH
 SMEM = pl.BlockSpec(memory_space=pltpu.SMEM)
 VMEM = pl.BlockSpec(memory_space=pltpu.VMEM)
+ANY = pl.BlockSpec(memory_space=pl.ANY)
+BUDGET = 58 << 20
 
 
 def iota(shape, dim):
@@ -51,6 +53,15 @@
         pair = ref[:, p * PAIR : (p + 1) * PAIR].astype(F32)
         columns += [pair[:, :C], pair[:, C:]]
     return columns
+
+
+def packed(rows):
+    return jnp.concatenate([rows[:144], rows[144:]], axis=1).astype(BF16)
+
+
+def unpacked(ref):
+    both = ref[...].astype(F32)
+    return jnp.concatenate([both[:, :C], both[:, C:]], axis=0).astype(BF16)
 
 
 def band_cells(tile_len):
@@ -71,8 +82,22 @@
 
 
 def bands_kernel(
-    rows_ref, step_ref, code_ref, shift_ref, x_ref, halo_ref, own, from_lo, from_hi, send, recv
+    rows_ref,
+    step_ref,
+    code_ref,
+    shift_ref,
+    x_hbm,
+    halo_ref,
+    x_ref,
+    own,
+    from_lo,
+    from_hi,
+    load,
+    send,
+    recv,
 ):
+    load_x = pltpu.make_async_copy(x_hbm, x_ref, load)
+    load_x.start()
     me = lax.axis_index("space")
     dp = lax.axis_index("dp")
     hi = lax.rem(me + 1, TILES)
@@ -80,9 +105,13 @@
     barrier = pltpu.get_barrier_semaphore()
     for peer in (lo, hi):
         pl.semaphore_signal(barrier, inc=1, device_id=(dp, peer), device_id_type=MESH)
+    wanted = jnp.concatenate(band_cells(rows_ref[me]), axis=0)
+    pick = one_hot(iota((288, CELLS), 1), wanted)
+    load_x.wait()
     cells = jnp.concatenate(columns_of(x_ref), axis=0).astype(BF16)
-    wanted = jnp.concatenate(band_cells(rows_ref[me]), axis=0)
-    own[...] = dot(one_hot(iota((288, CELLS), 1), wanted), cells).astype(BF16)
+    bands = dot(pick, cells)
+    own[...] = packed(bands)
+    bands = bands.astype(BF16)
     pl.semaphore_wait(barrier, 2)
     copies = []
     for n, (peer, landing) in enumerate(((hi, from_lo), (lo, from_hi))):
@@ -108,12 +137,11 @@
         picks.append(one_hot(iota((96, 96), 1), jnp.concatenate(parts, axis=0)))
     for copy in copies:
         copy.wait()
+    below, above = unpacked(from_lo), unpacked(from_hi)
     for k in range(3):
         rows = slice(96 * k, 96 * k + 96)
         halo_ref[rows, :] = (
-            dot(picks[0], from_lo[rows, :])
-            + dot(picks[1], own[rows, :])
-            + dot(picks[2], from_hi[rows, :])
+            dot(picks[0], below[rows]) + dot(picks[1], bands[rows]) + dot(picks[2], above[rows])
         ).astype(BF16)
 
 
@@ -122,21 +150,26 @@
     step_ref,
     code_ref,
     shift_ref,
-    x_ref,
-    c_ref,
+    x_hbm,
+    c_hbm,
     halo_ref,
     kern_ref,
     bias_ref,
     gain_ref,
     nbias_ref,
-    we_ref,
+    we_hbm,
     be_ref,
-    wp_ref,
+    wp_hbm,
     bp_ref,
     ls_ref,
     out_ref,
     ig_ref,
     wg_ref,
+    x_ref,
+    c_ref,
+    we_ref,
+    wp_ref,
+    load,
     weights,
     ext,
     ext_at,
@@ -179,6 +212,14 @@
     z_send,
     z_recv,
 ):
+    loads = [
+        pltpu.make_async_copy(source, landing, load.at[n])
+        for n, (source, landing) in enumerate(
+            ((x_hbm, x_ref), (c_hbm, c_ref), (we_hbm, we_ref), (wp_hbm, wp_ref))
+        )
+    ]
+    for copy in loads:
+        copy.start()
     me = lax.axis_index("space")
     dp = lax.axis_index("dp")
     mx = dp // 4
@@ -237,6 +278,7 @@
         ext[27 + k] = blank
         ext[2 - k, 8:32] = halo[96 * k + 48 : 96 * k + 72]
         ext[27 + k, 8:32] = halo[96 * k + 72 : 96 * k + 96]
+    loads[0].wait()
     for j, column in enumerate(columns_of(x_ref)):
         ext[3 + j, 8:32] += jnp.where(inside, column, 0.0)
 
@@ -271,6 +313,8 @@
         rstd[rows, :] = jnp.broadcast_to(inverse, (96, 128))
         normed[rows, :] = (scaled * gain_ref[...] + nbias_ref[...]).astype(BF16)
 
+    for copy in loads[1:]:
+        copy.wait()
     grads = [jnp.where(inside, column, 0.0) for column in columns_of(c_ref)]
     for j in range(TS):
         base_ref[j * TS : j * TS + TS, :] = grads[j]
@@ -393,7 +437,9 @@
             d_ext[2 - k, 3:27],
             d_ext[27 + k, 3:27],
         ]
-    dh_ref[...] = jnp.concatenate(parts, axis=0).astype(BF16)
+    own_dh = jnp.concatenate(parts, axis=0)
+    dh_ref[...] = packed(own_dh)
+    own_dh = own_dh.astype(BF16)
     dh_copies = [
         remote(dh_ref, dh_lo, dh_send.at[0], dh_recv.at[0], (dp, hi)),
         remote(dh_ref, dh_hi, dh_send.at[1], dh_recv.at[1], (dp, lo)),
@@ -486,13 +532,12 @@
 
     for copy in dh_copies:
         copy.wait()
+    below, above = unpacked(dh_lo), unpacked(dh_hi)
     parts = []
     for k in range(3):
         rows = slice(96 * k, 96 * k + 96)
         parts.append(
-            dot(spread[0], dh_lo[rows, :])
-            + dot(spread[1], dh_ref[rows, :])
-            + dot(spread[2], dh_hi[rows, :])
+            dot(spread[0], below[rows]) + dot(spread[1], own_dh[rows]) + dot(spread[2], above[rows])
         )
     d_bands = jnp.concatenate(parts, axis=0)
     upper = d_bands.astype(BF16)
@@ -520,6 +565,18 @@
         @pl.when(x >= 2)
         def _():
             x_copy(n, x, False).wait_send()
+
+
+def emit_kernel(out_ref, ig_ref, wg_ref, out_hbm, ig_hbm, wg_hbm, sems):
+    pairs = ((out_ref, out_hbm), (ig_ref, ig_hbm), (wg_ref.at[0], wg_hbm))
+    copies = [
+        pltpu.make_async_copy(source, landing, sems.at[n])
+        for n, (source, landing) in enumerate(pairs)
+    ]
+    for copy in copies:
+        copy.start()
+    for copy in copies:
+        copy.wait()
 
 
 def local(
@@ -546,11 +603,13 @@
     halo = pl.pallas_call(
         bands_kernel,
         out_shape=jax.ShapeDtypeStruct((288, C), BF16),
-        in_specs=[SMEM] * 4 + [VMEM],
+        in_specs=[SMEM] * 4 + [ANY],
         out_specs=VMEM,
-        scratch_shapes=[pltpu.VMEM((288, C), BF16)] * 3 + [dma((2,)), dma((2,))],
+        scratch_shapes=[pltpu.VMEM((TS, WIDE), BF16)]
+        + [pltpu.VMEM((144, PAIR), BF16)] * 3
+        + [dma, dma((2,)), dma((2,))],
         compiler_params=pltpu.CompilerParams(
-            collective_id=0, has_side_effects=True, vmem_limit_bytes=16 << 20
+            collective_id=0, has_side_effects=True, vmem_limit_bytes=BUDGET
         ),
         name="bands",
     )(tile_rows, *tables, x)
@@ -562,9 +621,17 @@
             jax.ShapeDtypeStruct((TS, WIDE), BF16),
             jax.ShapeDtypeStruct((1, 288), F32),
         ),
-        in_specs=[SMEM] * 4 + [VMEM] * 12,
+        in_specs=[SMEM] * 4
+        + [ANY, ANY]
+        + [VMEM] * 5
+        + [ANY, VMEM, ANY, VMEM, VMEM],
         out_specs=(VMEM,) * 3,
         scratch_shapes=[
+            vm((TS, WIDE), BF16),
+            vm((TS, WIDE), BF16),
+            vm((C, H), BF16),
+            vm((C, H), BF16),
+            dma((4,)),
             vm((49, 8, C), F32),
             vm((30, 40, C), F32),
             vm((7, 30, TS, C), F32),
@@ -579,11 +646,11 @@
             vm((7, 36, 32, C), F32),
             vm((30, 32, C), F32),
             vm((CELLS, C), F32),
-            vm((288, C), BF16),
+            vm((144, PAIR), BF16),
             vm((2, 2, 48, H), BF16),
             vm((2, 2, 96, PAIR), BF16),
-            vm((288, C), BF16),
-            vm((288, C), BF16),
+            vm((144, PAIR), BF16),
+            vm((144, PAIR), BF16),
             vm((2, 48, H), BF16),
             vm((2, 96, PAIR), BF16),
             vm((2, 48, H), BF16),
@@ -601,7 +668,7 @@
         + [dma((3,))] * 4
         + [dma] * 2,
         compiler_params=pltpu.CompilerParams(
-            collective_id=1, has_side_effects=True, vmem_limit_bytes=52 << 20
+            collective_id=1, has_side_effects=True, vmem_limit_bytes=BUDGET
         ),
         name="main",
     )(
@@ -620,11 +687,19 @@
         b_project.reshape(1, C),
         layer_scale.reshape(1, C),
     )
-    return (
-        out.reshape(1, 1, TS, WIDE),
-        ig.reshape(1, 1, TS, WIDE),
-        wg.reshape(288),
-    )
+    out, ig, wg = pl.pallas_call(
+        emit_kernel,
+        out_shape=(
+            jax.ShapeDtypeStruct((TS, WIDE), BF16),
+            jax.ShapeDtypeStruct((TS, WIDE), BF16),
+            jax.ShapeDtypeStruct((288,), F32),
+        ),
+        in_specs=[VMEM] * 3,
+        out_specs=(ANY,) * 3,
+        scratch_shapes=[dma((3,))],
+        name="emit",
+    )(out, ig, wg)
+    return out.reshape(1, 1, TS, WIDE), ig.reshape(1, 1, TS, WIDE), wg
 
 
 def solution(mesh):

time: 70.9 us -> 67.2 us (0.948)
  local copies, waits for them, and re-layouts: 5.87 us -> 0 us
  Pallas kernels: 63.3 us -> 66.3 us
    unnamed x34 -> x0, local copies, waits for them, and re-layouts: 5.87 us -> none
    pallas_call x0 -> x1, Pallas kernels: none -> 1.83 us  [local(): pl.pallas_call(emit_kernel, out_shape=(jax.ShapeDtypeStruct((TS, WIDE), B...]
where the time goes in v3:
time: 67.2 us; the launch traced here: 66.9 us
  Pallas kernels  66.3 us (99%)
    pallas_call x1, Pallas kernels, local(): pl.pallas_call(main_kernel, out_shape=(jax.ShapeDtypeStruct((TS, WIDE), B...  38 us
    pallas_call x1, Pallas kernels, local(): pl.pallas_call(bands_kernel, out_shape=jax.ShapeDtypeStruct((288, C), BF1...  26.5 us
    pallas_call x1, Pallas kernels, local(): pl.pallas_call(emit_kernel, out_shape=(jax.ShapeDtypeStruct((TS, WIDE), B...  1.83 us

profile of v3, /device:TPU:2, one launch (start us, length us, event | category | flops | bytes accessed | tf_op | source)
XLA Modules:
  0.0 66.9 jit_solution(4472075630269829969)
XLA Ops:
  0.6 26.5 %bands.1.halo_ref = bf16[288,192]{1,0:T(8,128)(2,1)} custom-call(s32[64]{0:T(128)} %rows_ref.3, s32[4,64]{1,0:T(4,128)} %bitcast.17, s32[4,64]{1,0:T(4,128)} %bitcast.19, s32[4,64]{1,0:T(4,128)} %bitcast.21, bf16[24,4608]{1,0:T(8,128)(2,1)} %bitcast.13), custom_call_target="tpu_custom_call" | custom-call | tf_op jit(solution)/shard_map/bands/pallas_call | solution.py:603
  27.1 38.0 %main.1 = (bf16[24,4608]{1,0:T(8,128)(2,1)}, bf16[24,4608]{1,0:T(8,128)(2,1)}, f32[1,288]{1,0:T(1,128)}) custom-call(s32[64]{0:T(128)} %rows_ref.3, s32[4,64]{1,0:T(4,128)} %bitcast.18, s32[4,64]{1,0:T(4,128)} %bitcast.20, s32[4,64]{1,0:T(4,128)} %bitcast.22, bf16[24,4608]{1,0:T(8,128)(2,1)} %bitcast.14, bf16[24,4608]{1,0:T(8,128)(2,1)} %bitcast.16, ...), custom_call_target="tpu_custom_call" | custom-call | tf_op jit(solution)/shard_map/main/pallas_call | solution.py:617
  65.1 1.8 %emit.1 = (bf16[24,4608]{1,0:T(8,128)(2,1)}, bf16[24,4608]{1,0:T(8,128)(2,1)}, f32[288]{0:T(512)}) custom-call(bf16[24,4608]{1,0:T(8,128)(2,1)} %get-tuple-element.9.out_ref, bf16[24,4608]{1,0:T(8,128)(2,1)} %get-tuple-element.10.ig_ref, f32[1,288]{1,0:T(1,128)} %get-tuple-element.11.wg_ref), custom_call_target="tpu_custom_call" | custom-call | tf_op jit(solution)/shard_map/emit/pallas_call | solution.py:690

commit v4 on v3

--- a/solution.py
+++ b/solution.py
@@ -87,7 +87,12 @@
     code_ref,
     shift_ref,
     x_hbm,
+    kern_ref,
+    bias_ref,
     halo_ref,
+    mixed_ref,
+    weights,
+    ext_at,
     x_ref,
     own,
     from_lo,
@@ -135,6 +140,36 @@
             first = jnp.where(step_ref[q, me] + 1 == source, (code // 2) * TS, -1000)
             parts.append(jnp.where(on_band, first + index, -1))
         picks.append(one_hot(iota((96, 96), 1), jnp.concatenate(parts, axis=0)))
+    tile_len = rows_ref[me]
+    inside = iota((TS, C), 0) < tile_len
+    for t in range(49):
+        weights[t] = jnp.broadcast_to(kern_ref[t // 7, t % 7 : t % 7 + 1, :], (8, C))
+    blank = jnp.zeros((7, TS, C), F32)
+    for k in range(3):
+        ext_at[:, k] = blank
+        ext_at[:, 27 + k] = blank
+    for j, column in enumerate(columns_of(x_ref)):
+        whole = jnp.concatenate(
+            [blank[0, :8], jnp.where(inside, column, 0.0), blank[0, :8]], axis=0
+        )
+        for a in range(7):
+            ext_at[a, 3 + j] = whole[5 + a : 29 + a]
+
+    @pl.loop(0, 6)
+    def _(block):
+        first = block * 4
+        totals = [jnp.broadcast_to(bias_ref[...], (TS, C)) for _ in range(4)]
+        for a in range(7):
+            for column in range(10):
+                value = ext_at[a, first + column].reshape(3, 8, C)
+                for j in range(4):
+                    b = column - j
+                    if 0 <= b < 7:
+                        totals[j] = totals[j] + (value * weights[7 * a + b][None]).reshape(TS, C)
+        for j in range(4):
+            at = pl.multiple_of((first + j) * TS, TS)
+            mixed_ref[pl.ds(at, TS), :] = totals[j]
+
     for copy in copies:
         copy.wait()
     below, above = unpacked(from_lo), unpacked(from_hi)
@@ -153,8 +188,8 @@
     x_hbm,
     c_hbm,
     halo_ref,
+    field_mixed,
     kern_ref,
-    bias_ref,
     gain_ref,
     nbias_ref,
     we_hbm,
@@ -171,8 +206,6 @@
     wp_ref,
     load,
     weights,
-    ext,
-    ext_at,
     mixed,
     normal,
     rstd,
@@ -211,6 +244,8 @@
     y_recv,
     z_send,
     z_recv,
+    near_sem,
+    far_sem,
 ):
     loads = [
         pltpu.make_async_copy(source, landing, load.at[n])
@@ -243,7 +278,9 @@
     ys = [lax.rem(my + d, 4) for d in (1, 2, 3)]
     far_first = sorted(range(1, 32), key=lambda d: -min(d, 32 - d))
     zs = [lax.rem(z + d, 32) for d in far_first]
-    peers = [at_z(other_z) for other_z in zs] + [at_y(y) for y in ys] + [at_x(x) for x in xs]
+    near = [at_z(lax.rem(z + d, 32)) for d in (4, 28, 3, 29, 2, 30, 1, 31)]
+    far = [at_z(lax.rem(z + d, 32)) for d in (8, 24)]
+    peers = near + [at_y(y) for y in ys] + [at_x(x) for x in xs]
     peers += [(dp, lo), (dp, hi), (other, me)]
     barrier = pltpu.get_barrier_semaphore()
     for peer in peers:
@@ -265,42 +302,48 @@
         weights[t] = jnp.broadcast_to(kern_ref[t // 7, t % 7 : t % 7 + 1, :], (8, C))
 
     halo = halo_ref[...].astype(F32)
+    blank = jnp.zeros((8, C), F32)
+
+    def framed(first):
+        return jnp.concatenate([blank, halo[first : first + TS], blank], axis=0)
+
+    sides = []
+    for q in (2, 3):
+        totals = [jnp.zeros((TS, C), F32) for _ in range(3)]
+        for k in range(3):
+            whole = framed(96 * k + TS * q)
+            at = 2 - k if q == 2 else 27 + k
+            for a in range(7):
+                value = whole[5 + a : 29 + a].reshape(3, 8, C)
+                for n in range(3):
+                    b = at - (n if q == 2 else 21 + n)
+                    if 0 <= b < 7:
+                        totals[n] = totals[n] + (value * weights[7 * a + b][None]).reshape(TS, C)
+        sides.append(jnp.concatenate(totals, axis=0))
+    lines = []
+    for q in (0, 1):
+        totals = [jnp.zeros((TS, C), F32) for _ in range(3)]
+        for k in range(3):
+            whole = framed(96 * k + TS * q)
+            for b in range(7):
+                value = whole[5 + b : 29 + b].reshape(3, 8, C)
+                for n in range(3):
+                    a = 2 - k - n if q == 0 else 6 + k - n
+                    if 0 <= a < 7:
+                        totals[n] = totals[n] + (value * weights[7 * a + b][None]).reshape(TS, C)
+        lines += totals
+    lines = jnp.concatenate(lines, axis=0)
+    upper = lines.astype(BF16)
+    lower = (lines - upper.astype(F32)).astype(BF16)
     col = iota((1, 144), 1)
-    target = col
-    for m in range(6):
-        row = (7 - m // 2) if m % 2 == 0 else (tile_len + 8 + m // 2)
-        target = jnp.where(col >= TS * m, col * 40 + (row - 960 * m), target)
-    edge_rows = jnp.concatenate([halo[96 * k : 96 * k + 48] for k in range(3)], axis=0).astype(BF16)
-    ext[3:27] = dot(one_hot(iota((960, 144), 0), target), edge_rows).reshape(TS, 40, C)
-    blank = jnp.zeros((40, C), F32)
-    for k in range(3):
-        ext[2 - k] = blank
-        ext[27 + k] = blank
-        ext[2 - k, 8:32] = halo[96 * k + 48 : 96 * k + 72]
-        ext[27 + k, 8:32] = halo[96 * k + 72 : 96 * k + 96]
-    loads[0].wait()
-    for j, column in enumerate(columns_of(x_ref)):
-        ext[3 + j, 8:32] += jnp.where(inside, column, 0.0)
-
-    @pl.loop(0, 30)
-    def _(at):
-        whole = ext[at]
-        for a in range(7):
-            ext_at[a, at] = whole[5 + a : 29 + a]
-
-    @pl.loop(0, 6)
-    def _(block):
-        first = block * 4
-        totals = [jnp.broadcast_to(bias_ref[...], (TS, C)) for _ in range(4)]
-        for a in range(7):
-            for column in range(10):
-                value = ext_at[a, first + column].reshape(3, 8, C)
-                for j in range(4):
-                    b = column - j
-                    if 0 <= b < 7:
-                        totals[j] = totals[j] + (value * weights[7 * a + b][None]).reshape(TS, C)
-        for j in range(4):
-            mixed[pl.ds((first + j) * TS, TS), :] = totals[j]
+    target = col * TS
+    for m in range(1, 6):
+        row = m if m < 3 else tile_len - 6 + m
+        target = jnp.where(col >= TS * m, (col - TS * m) * TS + row, target)
+    place = one_hot(iota((CELLS, 144), 0), target)
+    mixed[...] = field_mixed[...] + (dot(place, upper) + dot(place, lower))
+    mixed[0:72, :] += sides[0]
+    mixed[504:CELLS, :] += sides[1]
 
     @pl.loop(0, 6)
     def _(block):
@@ -313,7 +356,7 @@
         rstd[rows, :] = jnp.broadcast_to(inverse, (96, 128))
         normed[rows, :] = (scaled * gain_ref[...] + nbias_ref[...]).astype(BF16)
 
-    for copy in loads[1:]:
+    for copy in loads:
         copy.wait()
     grads = [jnp.where(inside, column, 0.0) for column in columns_of(c_ref)]
     for j in range(TS):
@@ -352,6 +395,8 @@
 
 
     pl.semaphore_wait(barrier, len(peers))
+    for peer in near:
+        pl.semaphore_signal(near_sem, inc=1, device_id=peer, device_id_type=MESH)
     core_copies = [
         remote(gi_ref.at[1 - core], core_i, core_send.at[0], core_recv.at[0], (other, me)),
         remote(gp_ref.at[1 - core], core_p, core_send.at[1], core_recv.at[1], (other, me)),
@@ -388,6 +433,10 @@
         own_x_p[x] = sum_p
         xs_i[x] = sum_i.astype(BF16)
         xs_p[x] = sum_p.astype(BF16)
+
+    pl.semaphore_wait(near_sem, len(near))
+    for peer in far:
+        pl.semaphore_signal(far_sem, inc=1, device_id=peer, device_id_type=MESH)
 
     def x_copy(n, x, wide):
         if wide:
@@ -527,6 +576,7 @@
         remote(z_send_buf.at[other_z], z_recv_buf.at[n], z_send, z_recv, at_z(other_z))
         for n, other_z in enumerate(zs)
     ]
+    pl.semaphore_wait(far_sem, len(far))
     for copy in z_copies:
         copy.start()
 
@@ -600,19 +650,26 @@
     c = cotangent.reshape(TS, WIDE)
     tables = (neighbour_step.T, neighbour_code.T, neighbour_shift.T)
     dma = pltpu.SemaphoreType.DMA
-    halo = pl.pallas_call(
+    halo, field_mixed = pl.pallas_call(
         bands_kernel,
-        out_shape=jax.ShapeDtypeStruct((288, C), BF16),
-        in_specs=[SMEM] * 4 + [ANY],
-        out_specs=VMEM,
-        scratch_shapes=[pltpu.VMEM((TS, WIDE), BF16)]
+        out_shape=(
+            jax.ShapeDtypeStruct((288, C), BF16),
+            jax.ShapeDtypeStruct((CELLS, C), F32),
+        ),
+        in_specs=[SMEM] * 4 + [ANY, VMEM, VMEM],
+        out_specs=(VMEM, VMEM),
+        scratch_shapes=[
+            pltpu.VMEM((49, 8, C), F32),
+            pltpu.VMEM((7, 30, TS, C), F32),
+            pltpu.VMEM((TS, WIDE), BF16),
+        ]
         + [pltpu.VMEM((144, PAIR), BF16)] * 3
         + [dma, dma((2,)), dma((2,))],
         compiler_params=pltpu.CompilerParams(
             collective_id=0, has_side_effects=True, vmem_limit_bytes=BUDGET
         ),
         name="bands",
-    )(tile_rows, *tables, x)
+    )(tile_rows, *tables, x, conv_kernel, conv_bias.reshape(1, C))
     vm = pltpu.VMEM
     out, ig, wg = pl.pallas_call(
         main_kernel,
@@ -633,8 +690,6 @@
             vm((C, H), BF16),
             dma((4,)),
             vm((49, 8, C), F32),
-            vm((30, 40, C), F32),
-            vm((7, 30, TS, C), F32),
             vm((CELLS, C), F32),
             vm((CELLS, C), F32),
             vm((CELLS, 128), F32),
@@ -666,7 +721,8 @@
         ]
         + [dma((2,))] * 4
         + [dma((3,))] * 4
-        + [dma] * 2,
+        + [dma] * 2
+        + [pltpu.SemaphoreType.REGULAR] * 2,
         compiler_params=pltpu.CompilerParams(
             collective_id=1, has_side_effects=True, vmem_limit_bytes=BUDGET
         ),
@@ -677,8 +733,8 @@
         x,
         c,
         halo,
+        field_mixed,
         conv_kernel,
-        conv_bias.reshape(1, C),
         norm_gain.reshape(1, C),
         norm_bias.reshape(1, C),
         w_expand,

time: 67.2 us -> 63.8 us (0.949)
  Pallas kernels: 66.3 us -> 62.9 us
    pallas_call x1, Pallas kernels: 38 us -> 34.6 us  [local(): pl.pallas_call(main_kernel, out_shape=(jax.ShapeDtypeStruct((TS, WIDE), B...]
where the time goes in v4:
time: 63.8 us; the launch traced here: 63.5 us
  Pallas kernels  62.9 us (99%)
  between operations  0.65 us (1%)
    pallas_call x1, Pallas kernels, local(): pl.pallas_call(main_kernel, out_shape=(jax.ShapeDtypeStruct((TS, WIDE), B...  34.6 us
    pallas_call x1, Pallas kernels, local(): pl.pallas_call(bands_kernel, out_shape=(jax.ShapeDtypeStruct((288, C), BF...  26.5 us
    pallas_call x1, Pallas kernels, local(): pl.pallas_call(emit_kernel, out_shape=(jax.ShapeDtypeStruct((TS, WIDE), B...  1.83 us

profile of v4, /device:TPU:2, one launch (start us, length us, event | category | flops | bytes accessed | tf_op | source)
XLA Modules:
  0.0 63.5 jit_solution(12554592115991186928)
XLA Ops:
  0.6 26.5 %bands.1 = (bf16[288,192]{1,0:T(8,128)(2,1)}, f32[576,192]{1,0:T(8,128)}) custom-call(s32[64]{0:T(128)} %rows_ref.3, s32[4,64]{1,0:T(4,128)} %bitcast.17, s32[4,64]{1,0:T(4,128)} %bitcast.19, s32[4,64]{1,0:T(4,128)} %bitcast.21, bf16[24,4608]{1,0:T(8,128)(2,1)} %bitcast.13, f32[7,7,192]{2,1,0:T(8,128)} %kern_ref.3, f32[1,192]{1,0:T(1,128)} %bitcast.27), custom_call_target="tpu_custom_call" | custom-call | tf_op jit(solution)/shard_map/bands/pallas_call | solution.py:653
  27.2 34.6 %main.1 = (bf16[24,4608]{1,0:T(8,128)(2,1)}, bf16[24,4608]{1,0:T(8,128)(2,1)}, f32[1,288]{1,0:T(1,128)}) custom-call(s32[64]{0:T(128)} %rows_ref.3, s32[4,64]{1,0:T(4,128)} %bitcast.18, s32[4,64]{1,0:T(4,128)} %bitcast.20, s32[4,64]{1,0:T(4,128)} %bitcast.22, bf16[24,4608]{1,0:T(8,128)(2,1)} %bitcast.14, bf16[24,4608]{1,0:T(8,128)(2,1)} %bitcast.16, ...), custom_call_target="tpu_custom_call" | custom-call | tf_op jit(solution)/shard_map/main/pallas_call | solution.py:674
  61.7 1.8 %emit.1 = (bf16[24,4608]{1,0:T(8,128)(2,1)}, bf16[24,4608]{1,0:T(8,128)(2,1)}, f32[288]{0:T(512)}) custom-call(bf16[24,4608]{1,0:T(8,128)(2,1)} %get-tuple-element.13.out_ref, bf16[24,4608]{1,0:T(8,128)(2,1)} %get-tuple-element.14.ig_ref, f32[1,288]{1,0:T(1,128)} %get-tuple-element.15.wg_ref), custom_call_target="tpu_custom_call" | custom-call | tf_op jit(solution)/shard_map/emit/pallas_call | solution.py:746

commit v5 on v4

--- a/solution.py
+++ b/solution.py
@@ -90,6 +90,7 @@
     kern_ref,
     bias_ref,
     halo_ref,
+    mixed_hbm,
     mixed_ref,
     weights,
     ext_at,
@@ -98,6 +99,7 @@
     from_lo,
     from_hi,
     load,
+    store,
     send,
     recv,
 ):
@@ -170,6 +172,8 @@
             at = pl.multiple_of((first + j) * TS, TS)
             mixed_ref[pl.ds(at, TS), :] = totals[j]
 
+    store_mixed = pltpu.make_async_copy(mixed_ref, mixed_hbm, store)
+    store_mixed.start()
     for copy in copies:
         copy.wait()
     below, above = unpacked(from_lo), unpacked(from_hi)
@@ -178,6 +182,7 @@
         halo_ref[rows, :] = (
             dot(picks[0], below[rows]) + dot(picks[1], bands[rows]) + dot(picks[2], above[rows])
         ).astype(BF16)
+    store_mixed.wait()
 
 
 def main_kernel(
@@ -197,9 +202,12 @@
     wp_hbm,
     bp_ref,
     ls_ref,
+    out_hbm,
+    ig_hbm,
+    wg_ref,
     out_ref,
     ig_ref,
-    wg_ref,
+    store,
     x_ref,
     c_ref,
     we_ref,
@@ -250,7 +258,13 @@
     loads = [
         pltpu.make_async_copy(source, landing, load.at[n])
         for n, (source, landing) in enumerate(
-            ((x_hbm, x_ref), (c_hbm, c_ref), (we_hbm, we_ref), (wp_hbm, wp_ref))
+            (
+                (field_mixed, mixed),
+                (x_hbm, x_ref),
+                (c_hbm, c_ref),
+                (we_hbm, we_ref),
+                (wp_hbm, wp_ref),
+            )
         )
     ]
     for copy in loads:
@@ -322,12 +336,12 @@
         sides.append(jnp.concatenate(totals, axis=0))
     lines = []
     for q in (0, 1):
-        totals = [jnp.zeros((TS, C), F32) for _ in range(3)]
+        totals = [jnp.zeros((TS, C), F32) for _ in range(3 if q == 0 else 9)]
         for k in range(3):
             whole = framed(96 * k + TS * q)
             for b in range(7):
                 value = whole[5 + b : 29 + b].reshape(3, 8, C)
-                for n in range(3):
+                for n in range(len(totals)):
                     a = 2 - k - n if q == 0 else 6 + k - n
                     if 0 <= a < 7:
                         totals[n] = totals[n] + (value * weights[7 * a + b][None]).reshape(TS, C)
@@ -335,13 +349,16 @@
     lines = jnp.concatenate(lines, axis=0)
     upper = lines.astype(BF16)
     lower = (lines - upper.astype(F32)).astype(BF16)
-    col = iota((1, 144), 1)
+    col = iota((1, 288), 1)
     target = col * TS
-    for m in range(1, 6):
+    for m in range(1, 12):
         row = m if m < 3 else tile_len - 6 + m
+        row = jnp.where(row < TS, row, -2 * CELLS)
         target = jnp.where(col >= TS * m, (col - TS * m) * TS + row, target)
-    place = one_hot(iota((CELLS, 144), 0), target)
-    mixed[...] = field_mixed[...] + (dot(place, upper) + dot(place, lower))
+    place = one_hot(iota((CELLS, 288), 0), target)
+    added = dot(place, upper) + dot(place, lower)
+    loads[0].wait()
+    mixed[...] += added
     mixed[0:72, :] += sides[0]
     mixed[504:CELLS, :] += sides[1]
 
@@ -356,7 +373,7 @@
         rstd[rows, :] = jnp.broadcast_to(inverse, (96, 128))
         normed[rows, :] = (scaled * gain_ref[...] + nbias_ref[...]).astype(BF16)
 
-    for copy in loads:
+    for copy in loads[1:]:
         copy.wait()
     grads = [jnp.where(inside, column, 0.0) for column in columns_of(c_ref)]
     for j in range(TS):
@@ -411,6 +428,8 @@
             pair.append(jnp.where(inside, column + ls_ref[...] * value, 0.0))
         out_ref[:, p * PAIR : (p + 1) * PAIR] = jnp.concatenate(pair, axis=1).astype(BF16)
 
+    store_out = pltpu.make_async_copy(out_ref, out_hbm, store.at[0])
+    store_out.start()
     d_pad[...] = jnp.zeros_like(d_pad)
 
     @pl.loop(0, 6)
@@ -600,11 +619,15 @@
             inside, jnp.concatenate(pair, axis=1), 0.0
         ).astype(BF16)
 
+    store_ig = pltpu.make_async_copy(ig_ref, ig_hbm, store.at[1])
+    store_ig.start()
     remote(z_recv_buf, z_recv_buf, z_send, z_recv, (other, me)).wait()
     total = z_send_buf[z].astype(F32)
     for n in range(31):
         total = total + z_recv_buf[n].astype(F32)
     wg_ref[...] = jnp.concatenate([total[t : t + 1] for t in range(3)], axis=1)
+    store_out.wait()
+    store_ig.wait()
 
     for n, x in enumerate(xs):
 
@@ -657,14 +680,15 @@
             jax.ShapeDtypeStruct((CELLS, C), F32),
         ),
         in_specs=[SMEM] * 4 + [ANY, VMEM, VMEM],
-        out_specs=(VMEM, VMEM),
+        out_specs=(VMEM, ANY),
         scratch_shapes=[
+            pltpu.VMEM((CELLS, C), F32),
             pltpu.VMEM((49, 8, C), F32),
             pltpu.VMEM((7, 30, TS, C), F32),
             pltpu.VMEM((TS, WIDE), BF16),
         ]
         + [pltpu.VMEM((144, PAIR), BF16)] * 3
-        + [dma, dma((2,)), dma((2,))],
+        + [dma, dma, dma((2,)), dma((2,))],
         compiler_params=pltpu.CompilerParams(
             collective_id=0, has_side_effects=True, vmem_limit_bytes=BUDGET
         ),
@@ -679,16 +703,19 @@
             jax.ShapeDtypeStruct((1, 288), F32),
         ),
         in_specs=[SMEM] * 4
-        + [ANY, ANY]
-        + [VMEM] * 5
+        + [ANY, ANY, VMEM, ANY]
+        + [VMEM] * 3
         + [ANY, VMEM, ANY, VMEM, VMEM],
-        out_specs=(VMEM,) * 3,
+        out_specs=(ANY, ANY, VMEM),
         scratch_shapes=[
+            vm((TS, WIDE), BF16),
+            vm((TS, WIDE), BF16),
+            dma((2,)),
             vm((TS, WIDE), BF16),
             vm((TS, WIDE), BF16),
             vm((C, H), BF16),
             vm((C, H), BF16),
-            dma((4,)),
+            dma((5,)),
             vm((49, 8, C), F32),
             vm((CELLS, C), F32),
             vm((CELLS, C), F32),

time: 63.8 us -> 64.5 us (1.011)
  no operation moved by 1% of the time
where the time goes in v5:
time: 64.5 us; the launch traced here: 64.2 us
  Pallas kernels  63.5 us (98%)
  between operations  0.65 us (1%)
    pallas_call x1, Pallas kernels, local(): pl.pallas_call(main_kernel, out_shape=(jax.ShapeDtypeStruct((TS, WIDE), B...  35.2 us
    pallas_call x1, Pallas kernels, local(): pl.pallas_call(bands_kernel, out_shape=(jax.ShapeDtypeStruct((288, C), BF...  26.5 us
    pallas_call x1, Pallas kernels, local(): pl.pallas_call(emit_kernel, out_shape=(jax.ShapeDtypeStruct((TS, WIDE), B...  1.83 us

profile of v5, /device:TPU:2, one launch (start us, length us, event | category | flops | bytes accessed | tf_op | source)
XLA Modules:
  0.0 64.2 jit_solution(16868308577937990820)
XLA Ops:
  0.6 26.5 %bands.1 = (bf16[288,192]{1,0:T(8,128)(2,1)}, f32[576,192]{1,0:T(8,128)}) custom-call(s32[64]{0:T(128)} %rows_ref.3, s32[4,64]{1,0:T(4,128)} %bitcast.17, s32[4,64]{1,0:T(4,128)} %bitcast.19, s32[4,64]{1,0:T(4,128)} %bitcast.21, bf16[24,4608]{1,0:T(8,128)(2,1)} %bitcast.13, f32[7,7,192]{2,1,0:T(8,128)} %kern_ref.3, f32[1,192]{1,0:T(1,128)} %bitcast.27), custom_call_target="tpu_custom_call" | custom-call | tf_op jit(solution)/shard_map/bands/pallas_call | solution.py:676
  27.2 35.2 %main.1 = (bf16[24,4608]{1,0:T(8,128)(2,1)}, bf16[24,4608]{1,0:T(8,128)(2,1)}, f32[1,288]{1,0:T(1,128)}) custom-call(s32[64]{0:T(128)} %rows_ref.3, s32[4,64]{1,0:T(4,128)} %bitcast.18, s32[4,64]{1,0:T(4,128)} %bitcast.20, s32[4,64]{1,0:T(4,128)} %bitcast.22, bf16[24,4608]{1,0:T(8,128)(2,1)} %bitcast.14, bf16[24,4608]{1,0:T(8,128)(2,1)} %bitcast.16, ...), custom_call_target="tpu_custom_call" | custom-call | tf_op jit(solution)/shard_map/main/pallas_call | solution.py:698
  62.4 1.8 %emit.1 = (bf16[24,4608]{1,0:T(8,128)(2,1)}, bf16[24,4608]{1,0:T(8,128)(2,1)}, f32[288]{0:T(512)}) custom-call(bf16[24,4608]{1,0:T(8,128)(2,1)} %get-tuple-element.13.out_ref, bf16[24,4608]{1,0:T(8,128)(2,1)} %get-tuple-element.14.ig_ref, f32[1,288]{1,0:T(1,128)} %get-tuple-element.15.wg_ref), custom_call_target="tpu_custom_call" | custom-call | tf_op jit(solution)/shard_map/emit/pallas_call | solution.py:773

commit v6 on v5

--- a/solution.py
+++ b/solution.py
@@ -478,8 +478,7 @@
         for a in range(7):
             d_at[a, at] = whole[8 - a : 40 - a]
 
-    @pl.loop(0, 10)
-    def _(block):
+    def convolve_back(block):
         first = block * 3
         totals = [jnp.zeros((32, C), F32) for _ in range(3)]
         for a in range(7):
@@ -492,28 +491,7 @@
         for j in range(3):
             d_ext[first + j] = totals[j]
 
-    parts = []
-    j = iota((TS, 1), 0)
-    for m in range(6):
-        parts.append(j * 32 + ((2 - m // 2) if m % 2 == 0 else (tile_len + 3 + m // 2)))
-    middle = d_ext[3:27].reshape(TS * 32, C).astype(BF16)
-    edge_rows = dot(one_hot(iota((144, TS * 32), 1), jnp.concatenate(parts, axis=0)), middle)
-    parts = []
-    for k in range(3):
-        parts += [
-            edge_rows[48 * k : 48 * k + 48],
-            d_ext[2 - k, 3:27],
-            d_ext[27 + k, 3:27],
-        ]
-    own_dh = jnp.concatenate(parts, axis=0)
-    dh_ref[...] = packed(own_dh)
-    own_dh = own_dh.astype(BF16)
-    dh_copies = [
-        remote(dh_ref, dh_lo, dh_send.at[0], dh_recv.at[0], (dp, hi)),
-        remote(dh_ref, dh_hi, dh_send.at[1], dh_recv.at[1], (dp, lo)),
-    ]
-    for copy in dh_copies:
-        copy.start()
+    pl.loop(0, 7)(convolve_back)
 
     def regroup(wide):
         if wide:
@@ -565,24 +543,31 @@
     for copy in y_copies:
         copy.start()
 
-    for j in range(TS):
-        base_ref[j * TS : j * TS + TS, :] += d_ext[3 + j, 3:27]
-
-
-    spread = []
-    lane = iota((1, 96), 1)
-    for source in range(3):
-        sender = lax.rem(me + source + TILES - 1, TILES)
-        target = jnp.full((1, 96), -1, jnp.int32)
-        for q in range(4):
-            code = code_ref[q, sender]
-            index, on_band = oriented(lane - TS * q, code, shift_ref[q, sender])
-            first = jnp.where(step_ref[q, sender] == 1 - source, (code // 2) * TS, -1000)
-            mine = (lane >= TS * q) & (lane < TS * q + TS)
-            target = jnp.where(mine & on_band, first + index, target)
-        spread.append(one_hot(iota((96, 96), 0), target))
-    cell = jnp.concatenate(band_cells(tile_len), axis=0)
-    to_bands = one_hot(iota((288, CELLS), 1), cell)
+    pl.loop(7, 10)(convolve_back)
+
+    parts = []
+    j = iota((TS, 1), 0)
+    for m in range(6):
+        parts.append(j * 32 + ((2 - m // 2) if m % 2 == 0 else (tile_len + 3 + m // 2)))
+    middle = d_ext[3:27].reshape(TS * 32, C).astype(BF16)
+    edge_rows = dot(one_hot(iota((144, TS * 32), 1), jnp.concatenate(parts, axis=0)), middle)
+    parts = []
+    for k in range(3):
+        parts += [
+            edge_rows[48 * k : 48 * k + 48],
+            d_ext[2 - k, 3:27],
+            d_ext[27 + k, 3:27],
+        ]
+    own_dh = jnp.concatenate(parts, axis=0)
+    dh_ref[...] = packed(own_dh)
+    own_dh = own_dh.astype(BF16)
+    dh_copies = [
+        remote(dh_ref, dh_lo, dh_send.at[0], dh_recv.at[0], (dp, hi)),
+        remote(dh_ref, dh_hi, dh_send.at[1], dh_recv.at[1], (dp, lo)),
+    ]
+    for copy in dh_copies:
+        copy.start()
+
     for copy in y_copies:
         copy.wait()
     total = y_send_buf[my].astype(F32)
@@ -599,6 +584,24 @@
     for copy in z_copies:
         copy.start()
 
+    for j in range(TS):
+        base_ref[j * TS : j * TS + TS, :] += d_ext[3 + j, 3:27]
+
+
+    spread = []
+    lane = iota((1, 96), 1)
+    for source in range(3):
+        sender = lax.rem(me + source + TILES - 1, TILES)
+        target = jnp.full((1, 96), -1, jnp.int32)
+        for q in range(4):
+            code = code_ref[q, sender]
+            index, on_band = oriented(lane - TS * q, code, shift_ref[q, sender])
+            first = jnp.where(step_ref[q, sender] == 1 - source, (code // 2) * TS, -1000)
+            mine = (lane >= TS * q) & (lane < TS * q + TS)
+            target = jnp.where(mine & on_band, first + index, target)
+        spread.append(one_hot(iota((96, 96), 0), target))
+    cell = jnp.concatenate(band_cells(tile_len), axis=0)
+    to_bands = one_hot(iota((288, CELLS), 1), cell)
     for copy in dh_copies:
         copy.wait()
     below, above = unpacked(dh_lo), unpacked(dh_hi)

time: 64.5 us -> 62.3 us (0.966)
  Pallas kernels: 63.5 us -> 61.4 us
    pallas_call x1, Pallas kernels: 35.2 us -> 33.1 us  [local(): pl.pallas_call(main_kernel, out_shape=(jax.ShapeDtypeStruct((TS, WIDE), B...]
where the time goes in v6:
time: 62.3 us; the launch traced here: 62.1 us
  Pallas kernels  61.4 us (99%)
  between operations  0.65 us (1%)
    pallas_call x1, Pallas kernels, local(): pl.pallas_call(main_kernel, out_shape=(jax.ShapeDtypeStruct((TS, WIDE), B...  33.1 us
    pallas_call x1, Pallas kernels, local(): pl.pallas_call(bands_kernel, out_shape=(jax.ShapeDtypeStruct((288, C), BF...  26.5 us
    pallas_call x1, Pallas kernels, local(): pl.pallas_call(emit_kernel, out_shape=(jax.ShapeDtypeStruct((TS, WIDE), B...  1.83 us

profile of v6, /device:TPU:2, one launch (start us, length us, event | category | flops | bytes accessed | tf_op | source)
XLA Modules:
  0.0 62.1 jit_solution(13995792047221004691)
XLA Ops:
  0.6 26.5 %bands.1 = (bf16[288,192]{1,0:T(8,128)(2,1)}, f32[576,192]{1,0:T(8,128)}) custom-call(s32[64]{0:T(128)} %rows_ref.3, s32[4,64]{1,0:T(4,128)} %bitcast.17, s32[4,64]{1,0:T(4,128)} %bitcast.19, s32[4,64]{1,0:T(4,128)} %bitcast.21, bf16[24,4608]{1,0:T(8,128)(2,1)} %bitcast.13, f32[7,7,192]{2,1,0:T(8,128)} %kern_ref.3, f32[1,192]{1,0:T(1,128)} %bitcast.27), custom_call_target="tpu_custom_call" | custom-call | tf_op jit(solution)/shard_map/bands/pallas_call | solution.py:679
  27.2 33.1 %main.1 = (bf16[24,4608]{1,0:T(8,128)(2,1)}, bf16[24,4608]{1,0:T(8,128)(2,1)}, f32[1,288]{1,0:T(1,128)}) custom-call(s32[64]{0:T(128)} %rows_ref.3, s32[4,64]{1,0:T(4,128)} %bitcast.18, s32[4,64]{1,0:T(4,128)} %bitcast.20, s32[4,64]{1,0:T(4,128)} %bitcast.22, bf16[24,4608]{1,0:T(8,128)(2,1)} %bitcast.14, bf16[24,4608]{1,0:T(8,128)(2,1)} %bitcast.16, ...), custom_call_target="tpu_custom_call" | custom-call | tf_op jit(solution)/shard_map/main/pallas_call | solution.py:701
  60.2 1.8 %emit.1 = (bf16[24,4608]{1,0:T(8,128)(2,1)}, bf16[24,4608]{1,0:T(8,128)(2,1)}, f32[288]{0:T(512)}) custom-call(bf16[24,4608]{1,0:T(8,128)(2,1)} %get-tuple-element.13.out_ref, bf16[24,4608]{1,0:T(8,128)(2,1)} %get-tuple-element.14.ig_ref, f32[1,288]{1,0:T(1,128)} %get-tuple-element.15.wg_ref), custom_call_target="tpu_custom_call" | custom-call | tf_op jit(solution)/shard_map/emit/pallas_call | solution.py:776
